TPU v7x, 32 devices: a whole 2x2x4 slice. The times are simulated.
32 devices in a mesh: groups: 2 (over x), ctx: 16 (over z, y, core).
Axes of the slice: x: 2, y: 2, z: 4, core: 2. Of those that a mesh axis runs over, the one named last changes fastest.
Arguments:
- queries: bfloat16 [8192, 1152], P(('groups', 'ctx')), parts along dimension 0, may hold values from -40 to 40
- keys: bfloat16 [8192, 1152], P(('groups', 'ctx')), parts along dimension 0, may hold values from -40 to 40
- values: bfloat16 [8192, 1152], P(('groups', 'ctx')), parts along dimension 0, may hold values from -6 to 6
- upstream: bfloat16 [8192, 1152], P(('groups', 'ctx')), parts along dimension 0, may hold values from -6 to 6
- lengths: int32 [12], P('groups'), parts along dimension 0, may hold values from 1 to 2, 8 in all
- modality: int32 [12], P('groups'), parts along dimension 0, may hold values from 0 to 1
- pairs: int32 [12], P('groups'), parts along dimension 0, may hold values from 0 to 5, as said below
- texts: float32 [12, 1152], P('groups'), parts along dimension 0, may hold values from -6 to 6
- modality_bias: float32 [2], replicated, may hold values from -12 to -4
Outputs:
- grad_queries: bfloat16 [8192, 1152], P(('groups', 'ctx')), parts along dimension 0
- grad_keys: bfloat16 [8192, 1152], P(('groups', 'ctx')), parts along dimension 0
- grad_values: bfloat16 [8192, 1152], P(('groups', 'ctx')), parts along dimension 0
- loss: float32 [12], P('groups'), parts along dimension 0
There are 2 independent parts, one for each index of `groups`. A program takes and returns all parts, laid end to end along the dimension named above; an argument that names none is the same for every part. Nothing has to cross between parts.
Inputs may be any that keep to these rules, and one draw needn't show every extreme that they name: `lengths`: the blocks of all scenes add up to 8, and some scene has 2 blocks. `pairs`: each caption belongs to exactly one scene.
All inputs are finite; a program needn't handle non-finite values.
Results may differ from a plain program's by a relative error of at most 0.0024.
The roundings to bfloat16 on the way count: a program that leaves them out, or rounds other values in their place, can miss the bound.
Values may be sent and summed in bfloat16 or wider, within the bound.
A program may use at most 128 MiB of HBM per device.

v0:
```python
import jax
import jax.numpy as jnp
from jax import lax
from jax.sharding import PartitionSpec as P

HEADS = 16
HEAD_DIM = 72
BLOCK = 512
REACH = 3


TEMPER = 10.0
LOSS_SCALE = 65536.0
EPSILON = 1e-06


def passed_along(shard, axis, by):
    size = lax.axis_size(axis)
    pairs = [(i, i + by) for i in range(size) if 0 <= i + by < size]
    return lax.ppermute(shard, axis, pairs)


def scene_of(positions, lengths, total):
    ends = jnp.cumsum(lengths) * BLOCK
    found = jnp.sum((positions[:, None] >= ends[None, :]).astype(jnp.int32), axis=1)
    inside = (positions >= 0) & (positions < total)
    return jnp.where(inside, found, -1)


def split_heads(x):
    return x.reshape(x.shape[0], HEADS, HEAD_DIM).transpose(1, 0, 2)


def join_heads(x):
    return x.transpose(1, 0, 2).reshape(x.shape[1], HEADS * HEAD_DIM)


def contrast(pooled_sum, lengths, modality, pairs, texts, modality_bias):
    count_rows = lengths.shape[0]
    sizes = (lengths * BLOCK).astype(jnp.float32)
    pooled = pooled_sum / sizes[:, None]
    norm = jnp.sqrt(jnp.sum(pooled * pooled, axis=1, keepdims=True) + EPSILON)
    unit = pooled / norm
    text_unit = texts / jnp.sqrt(jnp.sum(texts * texts, axis=1, keepdims=True) + EPSILON)
    bias = jnp.where(modality == 0, modality_bias[0], modality_bias[1])
    logits = TEMPER * jnp.dot(unit, text_unit.T, precision=lax.Precision.HIGHEST) + bias[:, None]
    labels = jnp.where(
        pairs[:, None] == jnp.arange(count_rows, dtype=jnp.int32)[None, :], 1.0, -1.0
    )
    margin = labels * logits
    loss = jnp.sum(jax.nn.softplus(-margin), axis=1)
    grad_logits = -labels * jax.nn.sigmoid(-margin) * (LOSS_SCALE / count_rows)
    grad_unit = TEMPER * jnp.dot(grad_logits, text_unit, precision=lax.Precision.HIGHEST)
    grad_pooled = (grad_unit - unit * jnp.sum(unit * grad_unit, axis=1, keepdims=True)) / norm
    return (loss, grad_pooled / sizes[:, None])


def tile_scores(q_heads, k_heads):
    scores = jnp.einsum("hqd,hkd->hqk", q_heads, k_heads, preferred_element_type=jnp.float32)
    return scores * HEAD_DIM ** (-0.5)


def tile_extent(mask, q_heads, k_heads):
    scores = tile_scores(q_heads, k_heads)
    allowed = mask[None]
    top = jnp.max(jnp.where(allowed, scores, -jnp.inf), axis=2)
    steady = jnp.where(jnp.isfinite(top), top, 0.0)
    total = jnp.sum(jnp.where(allowed, jnp.exp(scores - steady[:, :, None]), 0.0), axis=2)
    return (top, total)


def tile_output(mask, q_heads, k_heads, v_heads, lse):
    scores = tile_scores(q_heads, k_heads)
    probs = jnp.where(mask[None], jnp.exp(scores - lse[:, :, None]), 0.0).astype(jnp.bfloat16)
    return jnp.einsum("hqk,hkd->hqd", probs, v_heads, preferred_element_type=jnp.float32)


def tile_grads(mask, q_heads, grad_heads, lse, delta, k_heads, v_heads):
    scale = HEAD_DIM ** (-0.5)
    scores = tile_scores(q_heads, k_heads)
    probs = jnp.where(mask[None], jnp.exp(scores - lse[:, :, None]), 0.0)
    grad_probs = jnp.einsum("hqd,hkd->hqk", grad_heads, v_heads, preferred_element_type=jnp.float32)
    grad_scores = (probs * (grad_probs - delta[:, :, None])).astype(jnp.bfloat16)
    results = []
    results.append(
        jnp.einsum("hqk,hkd->hqd", grad_scores, k_heads, preferred_element_type=jnp.float32) * scale
    )
    results.append(
        jnp.einsum("hqk,hqd->hkd", grad_scores, q_heads, preferred_element_type=jnp.float32) * scale
    )
    results.append(
        jnp.einsum(
            "hqk,hqd->hkd",
            probs.astype(jnp.bfloat16),
            grad_heads,
            preferred_element_type=jnp.float32,
        )
    )
    return tuple(results)


def on_device(queries, keys, values, upstream, lengths, modality, pairs, texts, modality_bias):
    rows = queries.shape[0]
    total_rows = rows * lax.axis_size("ctx")
    place = lax.axis_index("ctx")
    base = place * rows + jnp.arange(rows, dtype=jnp.int32)
    own_scene = scene_of(base, lengths, total_rows)
    stacked = jnp.stack([keys, values])
    tiles = {0: stacked}
    for step in range(1, REACH + 1):
        for sign in (1, -1):
            tiles[-sign * step] = passed_along(stacked, "ctx", sign * step)
    offsets = list(range(-REACH, REACH + 1))
    others = [offset for offset in offsets if offset != 0]
    masks = {}
    head_tiles = {}
    for offset in offsets:
        far_scene = scene_of(base + offset * rows, lengths, total_rows)
        masks[offset] = own_scene[:, None] == far_scene[None, :]
        head_tiles[offset] = (split_heads(tiles[offset][0]), split_heads(tiles[offset][1]))
    q_heads = split_heads(queries)
    top, summed = tile_extent(masks[0], q_heads, head_tiles[0][0])
    for offset in others:
        part_top, part_sum = tile_extent(masks[offset], q_heads, head_tiles[offset][0])
        merged = jnp.maximum(top, part_top)
        summed = summed * jnp.exp(top - merged) + part_sum * jnp.exp(part_top - merged)
        top = merged
    lse = top + jnp.log(summed)
    attention_sum = jnp.zeros((HEADS, rows, HEAD_DIM), jnp.float32)
    for offset in offsets:
        attention_sum = attention_sum + tile_output(
            masks[offset], q_heads, head_tiles[offset][0], head_tiles[offset][1], lse
        )
    attended = join_heads(attention_sum).astype(jnp.bfloat16)
    scene_count = lengths.shape[0]
    member = own_scene[None, :] == jnp.arange(scene_count, dtype=jnp.int32)[:, None]
    partial_sums = jnp.dot(
        member.astype(jnp.bfloat16), attended, preferred_element_type=jnp.float32
    )
    pooled_sum = lax.psum(partial_sums, "ctx")
    loss, per_token = contrast(pooled_sum, lengths, modality, pairs, texts, modality_bias)
    scene_grad = jnp.take(per_token, own_scene, axis=0)
    grad_out = (upstream.astype(jnp.float32) + scene_grad).astype(jnp.bfloat16)
    grad_heads = split_heads(grad_out)
    delta = jnp.sum(
        grad_heads.astype(jnp.float32) * split_heads(attended).astype(jnp.float32), axis=2
    )
    own_parts = tile_grads(
        masks[0], q_heads, grad_heads, lse, delta, head_tiles[0][0], head_tiles[0][1]
    )
    grad_q = own_parts[0]
    grad_k = join_heads(own_parts[1])
    grad_v = join_heads(own_parts[2])
    for offset in others:
        near = tile_grads(
            masks[offset],
            q_heads,
            grad_heads,
            lse,
            delta,
            head_tiles[offset][0],
            head_tiles[offset][1],
        )
        grad_q = grad_q + near[0]
        returned = passed_along((join_heads(near[1]), join_heads(near[2])), "ctx", offset)
        grad_k = grad_k + returned[0]
        grad_v = grad_v + returned[1]
    return (
        join_heads(grad_q).astype(jnp.bfloat16),
        grad_k.astype(jnp.bfloat16),
        grad_v.astype(jnp.bfloat16),
        loss,
    )


def solution(mesh):
    in_specs = (
        P(("groups", "ctx"), None),
        P(("groups", "ctx"), None),
        P(("groups", "ctx"), None),
        P(("groups", "ctx"), None),
        P("groups"),
        P("groups"),
        P("groups"),
        P("groups", None),
        P(),
    )
    out_specs = (
        P(("groups", "ctx"), None),
        P(("groups", "ctx"), None),
        P(("groups", "ctx"), None),
        P("groups"),
    )
    return jax.shard_map(
        on_device, mesh=mesh, in_specs=in_specs, out_specs=out_specs, check_vma=False
    )
```

profile of v0, /device:TPU:25, one launch (start us, length us, event | category | flops | bytes accessed | tf_op | source)
XLA Modules:
  0.0 493.4 jit_solution(11662634360205901705)
XLA Ops:
  3.1 3.7 collective-permute-start.5
  10.9 3.5 collective-permute-start.2
  34.7 72.1 %collective-permute-done.4 = bf16[2,256,1152]{2,1,0:T(8,128)(2,1)} collective-permute-done((bf16[2,256,1152]{2,1,0:T(8,128)(2,1)}, bf16[2,256,1152]{2,1,0:T(8,128)(2,1)}, u32[]{:S(2)}, u32[]{:S(2)}) %collective-permute-start.4) | collective-permute-done | bytes 1179680 | tf_op jit(solution)/shard_map/ppermute | solution.py:20
  148.0 50.9 %psum.7 = f32[6,1152]{1,0:T(8,128)S(1)} all-reduce(f32[6,1152]{1,0:T(8,128)S(1)} %fusion.94), channel_id=1, replica_groups=mesh['groups'=2,'ctx'=16] {'ctx'}, use_global_device_ids=true, to_apply=%region_22.23 | all-reduce | flops 6912 | bytes 55296 | tf_op jit(solution)/shard_map/psum | solution.py:140
  205.4 4.4 fusion.68
  223.3 2.8 multiply_convert_fusion.2
  228.0 2.7 multiply_convert_fusion.3
  230.8 3.2 multiply_convert_fusion.4
  243.7 3.4 convolution_multiply_fusion.3
  249.8 3.4 convolution_multiply_fusion.4
  255.8 3.4 convolution_multiply_fusion.5
  273.6 5.7 %collective-permute-start.8 = (f32[256,1152]{1,0:T(8,128)}, f32[256,1152]{1,0:T(8,128)}, u32[]{:S(2)}, u32[]{:S(2)}) collective-permute-start(f32[256,1152]{1,0:T(8,128)} %copy.192), channel_id=1, source_target_pairs={{1,0},{2,1},{3,2},{4,3},{5,4},{6,5},{7,6},{8,7},{9,8},{10,9},{11,1... | collective-permute-start | bytes 3538952 | tf_op jit(solution)/shard_map/ppermute | solution.py:20
  281.3 3.3 fusion.153
  284.5 4.4 fusion.83
  289.0 2.8 multiply_convert_fusion.6
  291.8 4.5 collective-permute-done.6
  296.3 31.4 %collective-permute-start.10 = (f32[256,1152]{1,0:T(8,128)}, f32[256,1152]{1,0:T(8,128)}, u32[]{:S(2)}, u32[]{:S(2)}) collective-permute-start(f32[256,1152]{1,0:T(8,128)} %copy.196), channel_id=1, source_target_pairs={{0,2},{1,3},{2,4},{3,5},{4,6},{5,7},{6,8},{7,9},{8,10},{9,11},{10,... | collective-permute-start | bytes 3538952 | tf_op jit(solution)/shard_map/ppermute | solution.py:20
  349.5 40.8 %collective-permute-done.7 = f32[256,1152]{1,0:T(8,128)} collective-permute-done((f32[256,1152]{1,0:T(8,128)}, f32[256,1152]{1,0:T(8,128)}, u32[]{:S(2)}, u32[]{:S(2)}) %collective-permute-start.7) | collective-permute-done | bytes 1179680 | tf_op jit(solution)/shard_map/ppermute | solution.py:20
  392.2 11.7 %collective-permute-start.14 = (f32[256,1152]{1,0:T(8,128)}, f32[256,1152]{1,0:T(8,128)}, u32[]{:S(2)}, u32[]{:S(2)}) collective-permute-start(f32[256,1152]{1,0:T(8,128)} %copy.206), channel_id=1, source_target_pairs={{1,0},{2,1},{3,2},{4,3},{5,4},{6,5},{7,6},{8,7},{9,8},{10,9},{11,1... | collective-permute-start | bytes 3538952 | tf_op jit(solution)/shard_map/ppermute | solution.py:20
  403.9 4.6 collective-permute-start.15
  421.4 4.4 add_convert_fusion.1
  425.7 47.0 %collective-permute-done.13 = f32[256,1152]{1,0:T(8,128)} collective-permute-done((f32[256,1152]{1,0:T(8,128)}, f32[256,1152]{1,0:T(8,128)}, u32[]{:S(2)}, u32[]{:S(2)}) %collective-permute-start.13) | collective-permute-done | bytes 1179680 | tf_op jit(solution)/shard_map/ppermute | solution.py:20
  472.7 16.6 %collective-permute-done.14 = f32[256,1152]{1,0:T(8,128)} collective-permute-done((f32[256,1152]{1,0:T(8,128)}, f32[256,1152]{1,0:T(8,128)}, u32[]{:S(2)}, u32[]{:S(2)}) %collective-permute-start.14) | collective-permute-done | bytes 1179680 | tf_op jit(solution)/shard_map/ppermute | solution.py:20
  489.4 3.9 add_convert_fusion
  (294 shorter events, 157.0 us)
Async XLA Ops:
  3.1 29.7 %collective-permute-start.5 = (bf16[2,256,1152]{2,1,0:T(8,128)(2,1)}, bf16[2,256,1152]{2,1,0:T(8,128)(2,1)S(1)}, u32[]{:S(2)}, u32[]{:S(2)}) collective-permute-start(bf16[2,256,1152]{2,1,0:T(8,128)(2,1)} %pad_maximum_fusion), channel_id=1, source_target_pairs={{3,0},{4,1},{5,2},{6,3},{7,4},{8,5},{9,6},{10,7},{11,8},{12,9},{13... | collective-permute-start | bytes 3538952 | tf_op jit(solution)/shard_map/ppermute | solution.py:20
  6.7 100.1 %collective-permute-start.4 = (bf16[2,256,1152]{2,1,0:T(8,128)(2,1)}, bf16[2,256,1152]{2,1,0:T(8,128)(2,1)}, u32[]{:S(2)}, u32[]{:S(2)}) collective-permute-start(bf16[2,256,1152]{2,1,0:T(8,128)(2,1)} %pad_maximum_fusion), channel_id=1, source_target_pairs={{2,0},{3,1},{4,2},{5,3},{6,4},{7,5},{8,6},{9,7},{10,8},{11,9},{12,... | collective-permute-start | bytes 3538952 | tf_op jit(solution)/shard_map/ppermute | solution.py:20
  8.8 100.6 %collective-permute-start.3 = (bf16[2,256,1152]{2,1,0:T(8,128)(2,1)}, bf16[2,256,1152]{2,1,0:T(8,128)(2,1)}, u32[]{:S(2)}, u32[]{:S(2)}) collective-permute-start(bf16[2,256,1152]{2,1,0:T(8,128)(2,1)} %pad_maximum_fusion), channel_id=1, source_target_pairs={{1,0},{2,1},{3,2},{4,3},{5,4},{6,5},{7,6},{8,7},{9,8},{10,9},{11,1... | collective-permute-start | bytes 3538952 | tf_op jit(solution)/shard_map/ppermute | solution.py:20
  10.9 107.3 %collective-permute-start.2 = (bf16[2,256,1152]{2,1,0:T(8,128)(2,1)}, bf16[2,256,1152]{2,1,0:T(8,128)(2,1)}, u32[]{:S(2)}, u32[]{:S(2)}) collective-permute-start(bf16[2,256,1152]{2,1,0:T(8,128)(2,1)} %pad_maximum_fusion), channel_id=1, source_target_pairs={{0,1},{1,2},{2,3},{3,4},{4,5},{5,6},{6,7},{7,8},{8,9},{9,10},{10,1... | collective-permute-start | bytes 3538952 | tf_op jit(solution)/shard_map/ppermute | solution.py:20
  14.4 106.7 %collective-permute-start.1 = (bf16[2,256,1152]{2,1,0:T(8,128)(2,1)}, bf16[2,256,1152]{2,1,0:T(8,128)(2,1)}, u32[]{:S(2)}, u32[]{:S(2)}) collective-permute-start(bf16[2,256,1152]{2,1,0:T(8,128)(2,1)} %pad_maximum_fusion), channel_id=1, source_target_pairs={{0,2},{1,3},{2,4},{3,5},{4,6},{5,7},{6,8},{7,9},{8,10},{9,11},{10,... | collective-permute-start | bytes 3538952 | tf_op jit(solution)/shard_map/ppermute | solution.py:20
  32.7 91.3 %collective-permute-start = (bf16[2,256,1152]{2,1,0:T(8,128)(2,1)}, bf16[2,256,1152]{2,1,0:T(8,128)(2,1)}, u32[]{:S(2)}, u32[]{:S(2)}) collective-permute-start(bf16[2,256,1152]{2,1,0:T(8,128)(2,1)} %pad_maximum_fusion), channel_id=1, source_target_pairs={{0,3},{1,4},{2,5},{3,6},{4,7},{5,8},{6,9},{7,10},{8,11},{9,12},{10... | collective-permute-start | bytes 3538952 | tf_op jit(solution)/shard_map/ppermute | solution.py:20
  269.0 27.3 %collective-permute-start.6 = (f32[256,1152]{1,0:T(8,128)}, f32[256,1152]{1,0:T(8,128)S(1)}, u32[]{:S(2)}, u32[]{:S(2)}) collective-permute-start(f32[256,1152]{1,0:T(8,128)} %copy.187), channel_id=1, source_target_pairs={{3,0},{4,1},{5,2},{6,3},{7,4},{8,5},{9,6},{10,7},{11,8},{12,9},{13... | collective-permute-start | bytes 3538952 | tf_op jit(solution)/shard_map/ppermute | solution.py:20
  270.3 57.3 %collective-permute-start.12 = (f32[256,1152]{1,0:T(8,128)}, f32[256,1152]{1,0:T(8,128)S(1)}, u32[]{:S(2)}, u32[]{:S(2)}) collective-permute-start(f32[256,1152]{1,0:T(8,128)} %copy.201), channel_id=1, source_target_pairs={{3,0},{4,1},{5,2},{6,3},{7,4},{8,5},{9,6},{10,7},{11,8},{12,9},{13... | collective-permute-start | bytes 3538952 | tf_op jit(solution)/shard_map/ppermute | solution.py:20
  271.7 118.5 %collective-permute-start.7 = (f32[256,1152]{1,0:T(8,128)}, f32[256,1152]{1,0:T(8,128)}, u32[]{:S(2)}, u32[]{:S(2)}) collective-permute-start(f32[256,1152]{1,0:T(8,128)} %copy.190), channel_id=1, source_target_pairs={{2,0},{3,1},{4,2},{5,3},{6,4},{7,5},{8,6},{9,7},{10,8},{11,9},{12,... | collective-permute-start | bytes 3538952 | tf_op jit(solution)/shard_map/ppermute | solution.py:20
  273.6 118.5 %collective-permute-start.8 = (f32[256,1152]{1,0:T(8,128)}, f32[256,1152]{1,0:T(8,128)}, u32[]{:S(2)}, u32[]{:S(2)}) collective-permute-start(f32[256,1152]{1,0:T(8,128)} %copy.192), channel_id=1, source_target_pairs={{1,0},{2,1},{3,2},{4,3},{5,4},{6,5},{7,6},{8,7},{9,8},{10,9},{11,1... | collective-permute-start | bytes 3538952 | tf_op jit(solution)/shard_map/ppermute | solution.py:20
  279.4 124.5 %collective-permute-start.9 = (f32[256,1152]{1,0:T(8,128)}, f32[256,1152]{1,0:T(8,128)}, u32[]{:S(2)}, u32[]{:S(2)}) collective-permute-start(f32[256,1152]{1,0:T(8,128)} %copy.194), channel_id=1, source_target_pairs={{0,1},{1,2},{2,3},{3,4},{4,5},{5,6},{6,7},{7,8},{8,9},{9,10},{10,1... | collective-permute-start | bytes 3538952 | tf_op jit(solution)/shard_map/ppermute | solution.py:20
  296.3 112.2 %collective-permute-start.10 = (f32[256,1152]{1,0:T(8,128)}, f32[256,1152]{1,0:T(8,128)}, u32[]{:S(2)}, u32[]{:S(2)}) collective-permute-start(f32[256,1152]{1,0:T(8,128)} %copy.196), channel_id=1, source_target_pairs={{0,2},{1,3},{2,4},{3,5},{4,6},{5,7},{6,8},{7,9},{8,10},{9,11},{10,... | collective-permute-start | bytes 3538952 | tf_op jit(solution)/shard_map/ppermute | solution.py:20
  327.7 83.3 %collective-permute-start.11 = (f32[256,1152]{1,0:T(8,128)}, f32[256,1152]{1,0:T(8,128)}, u32[]{:S(2)}, u32[]{:S(2)}) collective-permute-start(f32[256,1152]{1,0:T(8,128)} %copy.198), channel_id=1, source_target_pairs={{0,3},{1,4},{2,5},{3,6},{4,7},{5,8},{6,9},{7,10},{8,11},{9,12},{10... | collective-permute-start | bytes 3538952 | tf_op jit(solution)/shard_map/ppermute | solution.py:20
  348.0 64.2 %copy-start.7 = (f32[16,256,256]{1,2,0:T(8,128)S(1)}, f32[16,256,256]{1,2,0:T(8,128)}, u32[]{:S(2)}) copy-start(f32[16,256,256]{1,2,0:T(8,128)} %copy-done.4) | copy-start | bytes 12582916
  348.0 64.2 %copy-start.41 = (bf16[256,1152]{0,1:T(8,128)(2,1)S(1)}, bf16[256,1152]{0,1:T(8,128)(2,1)}, u32[]{:S(2)}) copy-start(bf16[256,1152]{0,1:T(8,128)(2,1)} %copy-done.39) | copy-start | bytes 1769476
  349.4 67.4 %copy-start.38 = (bf16[16,256,72]{1,2,0:T(8,128)(2,1)S(1)}, bf16[16,256,72]{1,2,0:T(8,128)(2,1)}, u32[]{:S(2)}) copy-start(bf16[16,256,72]{1,2,0:T(8,128)(2,1)} %fusion.52) | copy-start | bytes 1769476
  349.5 68.5 %copy-start.16 = (bf16[16,256,256]{1,2,0:T(8,128)(2,1)S(1)}, bf16[16,256,256]{1,2,0:T(8,128)(2,1)}, u32[]{:S(2)}) copy-start(bf16[16,256,256]{1,2,0:T(8,128)(2,1)} %multiply_convert_fusion.6) | copy-start | bytes 6291460
  390.2 82.5 %collective-permute-start.13 = (f32[256,1152]{1,0:T(8,128)}, f32[256,1152]{1,0:T(8,128)}, u32[]{:S(2)}, u32[]{:S(2)}) collective-permute-start(f32[256,1152]{1,0:T(8,128)} %copy.204), channel_id=1, source_target_pairs={{2,0},{3,1},{4,2},{5,3},{6,4},{7,5},{8,6},{9,7},{10,8},{11,9},{12,... | collective-permute-start | bytes 3538952 | tf_op jit(solution)/shard_map/ppermute | solution.py:20
  392.2 97.2 %collective-permute-start.14 = (f32[256,1152]{1,0:T(8,128)}, f32[256,1152]{1,0:T(8,128)}, u32[]{:S(2)}, u32[]{:S(2)}) collective-permute-start(f32[256,1152]{1,0:T(8,128)} %copy.206), channel_id=1, source_target_pairs={{1,0},{2,1},{3,2},{4,3},{5,4},{6,5},{7,6},{8,7},{9,8},{10,9},{11,1... | collective-permute-start | bytes 3538952 | tf_op jit(solution)/shard_map/ppermute | solution.py:20
  403.9 85.5 %collective-permute-start.15 = (f32[256,1152]{1,0:T(8,128)}, f32[256,1152]{1,0:T(8,128)}, u32[]{:S(2)}, u32[]{:S(2)}) collective-permute-start(f32[256,1152]{1,0:T(8,128)} %copy.208), channel_id=1, source_target_pairs={{0,1},{1,2},{2,3},{3,4},{4,5},{5,6},{6,7},{7,8},{8,9},{9,10},{10,1... | collective-permute-start | bytes 3538952 | tf_op jit(solution)/shard_map/ppermute | solution.py:20
  408.5 80.9 %collective-permute-start.16 = (f32[256,1152]{1,0:T(8,128)}, f32[256,1152]{1,0:T(8,128)}, u32[]{:S(2)}, u32[]{:S(2)}) collective-permute-start(f32[256,1152]{1,0:T(8,128)} %copy.210), channel_id=1, source_target_pairs={{0,2},{1,3},{2,4},{3,5},{4,6},{5,7},{6,8},{7,9},{8,10},{9,11},{10,... | collective-permute-start | bytes 3538952 | tf_op jit(solution)/shard_map/ppermute | solution.py:20
  411.0 78.4 %collective-permute-start.17 = (f32[256,1152]{1,0:T(8,128)}, f32[256,1152]{1,0:T(8,128)}, u32[]{:S(2)}, u32[]{:S(2)}) collective-permute-start(f32[256,1152]{1,0:T(8,128)} %copy.212), channel_id=1, source_target_pairs={{0,3},{1,4},{2,5},{3,6},{4,7},{5,8},{6,9},{7,10},{8,11},{9,12},{10... | collective-permute-start | bytes 3538952 | tf_op jit(solution)/shard_map/ppermute | solution.py:20
  421.4 68.0 %copy-start.29 = (f32[256,1152]{1,0:T(8,128)S(1)}, f32[256,1152]{1,0:T(8,128)}, u32[]{:S(2)}) copy-start(f32[256,1152]{1,0:T(8,128)} %copy.202) | copy-start | bytes 3538948
  421.4 68.0 %copy-start.44 = (f32[256,1152]{1,0:T(8,128)S(1)}, f32[256,1152]{1,0:T(8,128)}, u32[]{:S(2)}) copy-start(f32[256,1152]{1,0:T(8,128)} %copy-done.43) | copy-start | bytes 3538948
  (71 other events, 706.7 us)
where the time goes:
time: 499 us; the launch traced here: 493 us
  waiting for transfers between devices  185 us (37%)
  starting transfers between devices  82.4 us (17%)
  matrix products  78.1 us (16%)
  local copies, waits for them, and re-layouts  68.3 us (14%)
  blocking collectives  50.9 us (10%)
  other arithmetic  26.8 us (5%)
    ppermute x18, waiting for transfers between devices, passed_along(): return lax.ppermute(shard, axis, pairs)  185 us
    ppermute x18, starting transfers between devices, passed_along(): return lax.ppermute(shard, axis, pairs)  82.4 us
    psum x1, blocking collectives, on_device(): pooled_sum = lax.psum(partial_sums, 'ctx')  50.9 us
    reshape x14, local copies, waits for them, and re-layouts, join_heads(): return x.transpose(1, 0, 2).reshape(x.shape[1], HEADS * HEAD_DIM)  36.4 us
    dot_general x7, matrix products, tile_grads(): jnp.einsum('hqk,hqd->hkd', probs.astype(jnp.bfloat16), grad_heads, prefer...  18.5 us
    dot_general x7, matrix products, tile_grads(): jnp.einsum('hqk,hqd->hkd', grad_scores, q_heads, preferred_element_type=j...  17.3 us
    dot_general x7, matrix products, tile_grads(): jnp.einsum('hqd,hkd->hqk', grad_heads, v_heads, preferred_element_type=jn...  16.9 us
    slice x12, local copies, waits for them, and re-layouts, on_device(): tiles[offset][1]  16.4 us
  transfers between devices with their start and end apart: 18, of which 7 were waited for; matrix products, arithmetic and copies ran while one was open for 15% of the time, Pallas kernels for 0%

commit v1 on v0

v1 whole, which is shorter than its diff:
```python
import jax
import jax.numpy as jnp
from jax import lax
from jax.experimental import pallas as pl
from jax.experimental.pallas import tpu as pltpu
from jax.sharding import PartitionSpec as P

HEADS = 16
HEAD_DIM = 72
BLOCK = 512
QUARTER = 4
CHUNK = 256
TEMPER = 10.0
LOSS_SCALE = 65536.0
EPSILON = 1e-06
SCALE = HEAD_DIM ** (-0.5)
LOG2E = 1.4426950408889634
FAR = -1e30


def dot_over(x, y, dim_x, dim_y):
    return lax.dot_general(
        x, y, (((dim_x,), (dim_y,)), ((), ())), preferred_element_type=jnp.float32
    )


def attend_kernel(far_ref, a_ref, b_ref, att_a, att_b, lse_a, lse_b, pool_ref):
    far = far_ref[0]
    sides = (a_ref, b_ref)
    lane = lax.broadcasted_iota(jnp.int32, (HEAD_DIM, 128), 1)
    pools = []
    for own in range(2):
        pool = jnp.zeros((HEAD_DIM, 1), jnp.float32)
        for start in range(0, BLOCK, CHUNK):
            q = sides[own][0, 0, :, start : start + CHUNK]
            scores = []
            for side in range(2):
                s = dot_over(sides[side][1, 0], q, 0, 0) * (SCALE * LOG2E)
                scores.append(s if side == own else s + far)
            top = jnp.maximum(
                jnp.max(scores[0], axis=0, keepdims=True),
                jnp.max(scores[1], axis=0, keepdims=True),
            )
            parts = [jnp.exp2(s - top) for s in scores]
            total = jnp.sum(parts[0], axis=0, keepdims=True) + jnp.sum(
                parts[1], axis=0, keepdims=True
            )
            scale = 1.0 / total
            att = jnp.zeros((HEAD_DIM, CHUNK), jnp.float32)
            for side in range(2):
                probs = (parts[side] * scale).astype(jnp.bfloat16)
                att = att + dot_over(sides[side][2, 0], probs, 1, 0)
            att = att.astype(jnp.bfloat16)
            (att_a, att_b)[own][0, :, start : start + CHUNK] = att
            (lse_a, lse_b)[own][0, :, start : start + CHUNK] = top + jnp.log2(total)
            pool = pool + jnp.sum(att.astype(jnp.float32), axis=1, keepdims=True)
        pools.append(pool)
    pool_ref[0] = jnp.where(lane == 0, pools[0], jnp.where(lane == 1, pools[1], 0.0))


def grads_kernel(
    far_ref, a_ref, b_ref, ua_ref, ub_ref, att_a, att_b, lse_a, lse_b, ga_ref, gb_ref,
    out_a, out_b, acc_ref,
):
    far = far_ref[0]
    sides = (a_ref, b_ref)
    outs = (out_a, out_b)
    first = True
    for own in range(2):
        for start in range(0, BLOCK, CHUNK):
            span = slice(start, start + CHUNK)
            q = sides[own][0, 0, :, span]
            up = (ua_ref, ub_ref)[own][0, :, span].astype(jnp.float32)
            grad = (up + (ga_ref, gb_ref)[own][0]).astype(jnp.bfloat16)
            att = (att_a, att_b)[own][0, :, span].astype(jnp.float32)
            lse = (lse_a, lse_b)[own][0, :, span]
            delta = jnp.sum(grad.astype(jnp.float32) * att, axis=0, keepdims=True)
            grad_q = jnp.zeros((HEAD_DIM, CHUNK), jnp.float32)
            for side in range(2):
                k = sides[side][1, 0]
                s = dot_over(k, q, 0, 0) * (SCALE * LOG2E)
                if side != own:
                    s = s + far
                probs = jnp.exp2(s - lse)
                grad_probs = dot_over(sides[side][2, 0], grad, 0, 0)
                grad_scores = (probs * (grad_probs - delta)).astype(jnp.bfloat16)
                grad_q = grad_q + dot_over(k, grad_scores, 1, 0)
                grad_k = dot_over(q, grad_scores, 1, 1)
                grad_v = dot_over(grad, probs.astype(jnp.bfloat16), 1, 1)
                if first:
                    acc_ref[side, 0] = grad_k
                    acc_ref[side, 1] = grad_v
                else:
                    acc_ref[side, 0] += grad_k
                    acc_ref[side, 1] += grad_v
            first = False
            outs[own][0, 0, :, span] = (grad_q * SCALE).astype(jnp.bfloat16)
    for side in range(2):
        outs[side][1, 0] = (acc_ref[side, 0] * SCALE).astype(jnp.bfloat16)
        outs[side][2, 0] = acc_ref[side, 1].astype(jnp.bfloat16)


def head_block(lead, rows, columns):
    if lead:
        return pl.BlockSpec((lead, 1, rows, columns), lambda h: (0, h, 0, 0))
    return pl.BlockSpec((1, rows, columns), lambda h: (h, 0, 0))


SMEM = pl.BlockSpec(memory_space=pltpu.SMEM)


def attend(far, a, b):
    tile = jax.ShapeDtypeStruct((QUARTER, HEAD_DIM, BLOCK), jnp.bfloat16)
    line = jax.ShapeDtypeStruct((QUARTER, 1, BLOCK), jnp.float32)
    return pl.pallas_call(
        attend_kernel,
        grid=(QUARTER,),
        in_specs=[SMEM, head_block(3, HEAD_DIM, BLOCK), head_block(3, HEAD_DIM, BLOCK)],
        out_specs=[
            head_block(0, HEAD_DIM, BLOCK),
            head_block(0, HEAD_DIM, BLOCK),
            head_block(0, 1, BLOCK),
            head_block(0, 1, BLOCK),
            head_block(0, HEAD_DIM, 128),
        ],
        out_shape=[
            tile, tile, line, line,
            jax.ShapeDtypeStruct((QUARTER, HEAD_DIM, 128), jnp.float32),
        ],
        compiler_params=pltpu.CompilerParams(vmem_limit_bytes=48 * 2**20),
        cost_estimate=pl.CostEstimate(
            flops=4 * QUARTER * HEAD_DIM * 4 * BLOCK * BLOCK,
            bytes_accessed=5 * 10**6,
            transcendentals=QUARTER * 4 * BLOCK * BLOCK,
        ),
        name="attend",
    )(far, a, b)


def grads(far, a, b, ua, ub, att_a, att_b, lse_a, lse_b, ga, gb):
    tile = jax.ShapeDtypeStruct((3, QUARTER, HEAD_DIM, BLOCK), jnp.bfloat16)
    wide = head_block(3, HEAD_DIM, BLOCK)
    one = head_block(0, HEAD_DIM, BLOCK)
    line = head_block(0, 1, BLOCK)
    column = head_block(0, HEAD_DIM, 1)
    return pl.pallas_call(
        grads_kernel,
        grid=(QUARTER,),
        in_specs=[SMEM, wide, wide, one, one, one, one, line, line, column, column],
        out_specs=[wide, wide],
        out_shape=[tile, tile],
        scratch_shapes=[pltpu.VMEM((2, 2, HEAD_DIM, BLOCK), jnp.float32)],
        compiler_params=pltpu.CompilerParams(vmem_limit_bytes=48 * 2**20),
        cost_estimate=pl.CostEstimate(
            flops=10 * QUARTER * HEAD_DIM * 4 * BLOCK * BLOCK,
            bytes_accessed=8 * 10**6,
            transcendentals=QUARTER * 4 * BLOCK * BLOCK,
        ),
        name="grads",
    )(far, a, b, ua, ub, att_a, att_b, lse_a, lse_b, ga, gb)


def contrast_row(pooled_sum, size, kind, pair, texts, modality_bias, count):
    pooled = pooled_sum / size
    norm = jnp.sqrt(jnp.sum(pooled * pooled) + EPSILON)
    unit = pooled / norm
    text_unit = texts / jnp.sqrt(jnp.sum(texts * texts, axis=1, keepdims=True) + EPSILON)
    bias = jnp.where(kind == 0, modality_bias[0], modality_bias[1])
    logits = TEMPER * jnp.sum(text_unit * unit[None, :], axis=1) + bias
    labels = jnp.where(pair == jnp.arange(count, dtype=jnp.int32), 1.0, -1.0)
    margin = labels * logits
    loss = jnp.sum(jax.nn.softplus(-margin))
    grad_logits = -labels * jax.nn.sigmoid(-margin) * (LOSS_SCALE / count)
    grad_unit = TEMPER * jnp.sum(grad_logits[:, None] * text_unit, axis=0)
    grad_pooled = (grad_unit - unit * jnp.sum(unit * grad_unit)) / norm
    return loss, grad_pooled / size


def on_device(queries, keys, values, upstream, lengths, modality, pairs, texts, modality_bias):
    rows = queries.shape[0]
    devices = lax.axis_size("ctx")
    count = lengths.shape[0]
    place = lax.axis_index("ctx")
    block, core = place // 2, place % 2
    ends = jnp.cumsum(lengths)
    scene = jnp.sum((block >= ends).astype(jnp.int32))
    length = lengths[scene]
    second = block - (ends[scene] - length)
    paired = length == 2
    beside = (block - second + (1 - second)) == (block ^ 1)
    far = jnp.where(paired, 0.0, FAR).astype(jnp.float32).reshape(1)

    def swap_core(x):
        return lax.ppermute(x, "ctx", [(i, i ^ 1) for i in range(devices)])

    def across(x):
        return lax.ppermute(x, "ctx", [(i, i ^ 2) for i in range(devices)])

    def relayed(x):
        hops = [(i, i - 4 if i & 2 else i + 4) for i in range(devices)]
        hops = [(i, j) for i, j in hops if 0 <= j < devices]
        return lax.ppermute(x, "ctx", hops)

    def partner(x):
        near = across(x)
        return jnp.where(beside, near, relayed(near))

    def widened(x):
        x = x.T.reshape(2, 2, QUARTER, HEAD_DIM, rows)
        mine = lax.dynamic_index_in_dim(x, core, 1, keepdims=False)
        return mine, lax.dynamic_index_in_dim(x, 1 - core, 1, keepdims=False)

    def own_block(arrays):
        pieces = [widened(x) for x in arrays]
        mine = jnp.stack([p[0] for p in pieces])
        theirs = swap_core(jnp.stack([p[1] for p in pieces]))
        whole = jnp.concatenate([mine, theirs], axis=4)
        return (
            lax.dynamic_index_in_dim(whole, second, 1, keepdims=False),
            lax.dynamic_index_in_dim(whole, 1 - second, 1, keepdims=False),
        )

    a, given = own_block((queries, keys, values))
    ua, u_given = own_block((upstream,))
    b = jnp.where(paired, partner(given), given)
    ub = jnp.where(paired, partner(u_given), u_given)
    att_a, att_b, lse_a, lse_b, pool = attend(far, a, b)

    width = QUARTER * HEAD_DIM
    pool_a, pool_b = pool[:, :, 0].reshape(width), pool[:, :, 1].reshape(width)
    half_of_a = jnp.where(paired, second, 0)
    mine = jnp.where(paired, pool_a + pool_b, pool_a)
    halves = jnp.arange(2, dtype=jnp.int32)
    by_half = jnp.where(
        halves[:, None] == half_of_a, mine[None], jnp.where(paired, 0.0, pool_b[None])
    )
    sums = jnp.where(halves[None, :, None] == core, by_half[:, None, :], 0.0)
    sums = sums + swap_core(sums)
    from_before = lax.ppermute(sums, "ctx", [(i, i + 2) for i in range(devices - 2)])
    from_after = lax.ppermute(sums, "ctx", [(i + 2, i) for i in range(devices - 2)])
    sums = sums + jnp.where(paired, jnp.where(second == 1, from_before, from_after), 0.0)
    size = (length * BLOCK).astype(jnp.float32)
    loss_here, per_token = contrast_row(
        sums.reshape(-1), size, modality[scene], pairs[scene], texts, modality_bias, count
    )
    speaks = (core == 0) & (second == 0)
    loss = jnp.where((jnp.arange(count) == scene) & speaks, loss_here, 0.0)
    loss = lax.psum(loss, "ctx")
    per_half = lax.dynamic_index_in_dim(
        per_token.reshape(2, 2, QUARTER, HEAD_DIM, 1), core, 1, keepdims=False
    )
    ga = jnp.where(half_of_a == 1, per_half[1], per_half[0])
    gb = jnp.where(paired, ga, per_half[1])
    out_a, out_b = grads(far, a, b, ua[0], ub[0], att_a, att_b, lse_a, lse_b, ga, gb)

    back = partner(out_b)
    low = jnp.where(paired & (second == 1), back, out_a)
    high = jnp.where(paired, jnp.where(second == 1, out_a, back), out_b)
    whole = jnp.stack([low, high])
    mine = whole[..., :rows]
    theirs = swap_core(whole[..., rows:])
    even = jnp.where(core == 0, mine, theirs)
    odd = jnp.where(core == 0, theirs, mine)
    done = jnp.stack([even, odd], axis=1)
    done = done.transpose(2, 5, 0, 1, 3, 4).reshape(3, rows, HEADS * HEAD_DIM)
    return done[0], done[1], done[2], loss


def solution(mesh):
    tokens = P(("groups", "ctx"), None)
    in_specs = (
        tokens, tokens, tokens, tokens,
        P("groups"), P("groups"), P("groups"), P("groups", None), P(),
    )
    out_specs = (tokens, tokens, tokens, P("groups"))
    return jax.shard_map(
        on_device, mesh=mesh, in_specs=in_specs, out_specs=out_specs, check_vma=False
    )
```

time: 499 us -> 192 us (0.38)
  the two profiles are of different devices: /device:TPU:25 before, /device:TPU:0 now
where the time goes in v1:
time: 192 us; the launch traced here: 191 us
  waiting for transfers between devices  70.3 us (37%)
  blocking collectives  32.5 us (17%)
  starting transfers between devices  25.1 us (13%)
  Pallas kernels  25 us (13%)
  local copies, waits for them, and re-layouts  17 us (9%)
  other arithmetic  12.9 us (7%)
  between operations  8.14 us (4%)
    ppermute x3, waiting for transfers between devices, across(): return lax.ppermute(x, 'ctx', [(i, i ^ 2) for i in range(devices)])  47.5 us
    psum x1, blocking collectives, on_device(): loss = lax.psum(loss, 'ctx')  32.5 us
    ppermute x3, waiting for transfers between devices, relayed(): return lax.ppermute(x, 'ctx', hops)  22.1 us
    pallas_call x1, Pallas kernels, grads(): pl.pallas_call(grads_kernel, grid=(QUARTER,), in_specs=[SMEM, wide, wide,...  14.2 us
    unnamed x45, local copies, waits for them, and re-layouts  12.3 us
    ppermute x3, starting transfers between devices, relayed(): return lax.ppermute(x, 'ctx', hops)  12.3 us
    pallas_call x1, Pallas kernels, attend(): pl.pallas_call(attend_kernel, grid=(QUARTER,), in_specs=[SMEM, head_block...  10.9 us
    ppermute x3, starting transfers between devices, across(): return lax.ppermute(x, 'ctx', [(i, i ^ 2) for i in range(devices)])  5.93 us
  transfers between devices with their start and end apart: 12, of which 7 were waited for; matrix products, arithmetic and copies ran while one was open for 5% of the time, Pallas kernels for 6%

profile of v1, /device:TPU:0, one launch (start us, length us, event | category | flops | bytes accessed | tf_op | source)
XLA Modules:
  0.0 191.0 jit_solution(15827609130426722144)
XLA Ops:
  0.7 1.4 copy.21
  2.0 1.3 copy.22
  10.0 3.0 %collective-permute-start.1 = (bf16[3,4,72,512]{3,2,1,0:T(8,128)(2,1)S(1)}, bf16[3,4,72,512]{3,2,1,0:T(8,128)(2,1)}, u32[]{:S(2)}, u32[]{:S(2)}) collective-permute-start(bf16[3,4,72,512]{3,2,1,0:T(8,128)(2,1)S(1)} %get-tuple-element.37), channel_id=1, source_target_pairs={{0,2},{1,3},{2,0},{3,1},{4,6},{5,7},{6,4},{7,5},{8,10},{9,11},{10,... | collective-permute-start | bytes 2654216 | tf_op jit(solution)/shard_map/ppermute | solution.py:197
  13.0 20.1 %collective-permute-done.1 = bf16[3,4,72,512]{3,2,1,0:T(8,128)(2,1)} collective-permute-done((bf16[3,4,72,512]{3,2,1,0:T(8,128)(2,1)S(1)}, bf16[3,4,72,512]{3,2,1,0:T(8,128)(2,1)}, u32[]{:S(2)}, u32[]{:S(2)}) %collective-permute-start.1) | collective-permute-done | bytes 884768 | tf_op jit(solution)/shard_map/ppermute | solution.py:197
  33.0 4.7 %collective-permute-start.2 = (bf16[3,4,72,512]{3,2,1,0:T(8,128)(2,1)}, bf16[3,4,72,512]{3,2,1,0:T(8,128)(2,1)}, u32[]{:S(2)}, u32[]{:S(2)}) collective-permute-start(bf16[3,4,72,512]{3,2,1,0:T(8,128)(2,1)} %collective-permute-done.1), channel_id=1, source_target_pairs={{0,4},{1,5},{4,8},{5,9},{6,2},{7,3},{8,12},{9,13},{10,6},{11,7},{1... | collective-permute-start | bytes 2654216 | tf_op jit(solution)/shard_map/ppermute | solution.py:202
  41.4 8.2 %collective-permute-done.4 = bf16[1,4,72,512]{3,2,1,0:T(8,128)(2,1)S(1)} collective-permute-done((bf16[1,4,72,512]{3,2,1,0:T(8,128)(2,1)S(1)}, bf16[1,4,72,512]{3,2,1,0:T(8,128)(2,1)S(1)}, u32[]{:S(2)}, u32[]{:S(2)}) %collective-permute-start.4) | collective-permute-done | bytes 294944 | tf_op jit(solution)/shard_map/ppermute | solution.py:197
  49.6 2.5 %collective-permute-start.5 = (bf16[1,4,72,512]{3,2,1,0:T(8,128)(2,1)S(1)}, bf16[1,4,72,512]{3,2,1,0:T(8,128)(2,1)S(1)}, u32[]{:S(2)}, u32[]{:S(2)}) collective-permute-start(bf16[1,4,72,512]{3,2,1,0:T(8,128)(2,1)S(1)} %collective-permute-done.4), channel_id=1, source_target_pairs={{0,4},{1,5},{4,8},{5,9},{6,2},{7,3},{8,12},{9,13},{10,6},{11,7},{1... | collective-permute-start | bytes 884744 | tf_op jit(solution)/shard_map/ppermute | solution.py:202
  52.2 4.9 %collective-permute-done.2 = bf16[3,4,72,512]{3,2,1,0:T(8,128)(2,1)} collective-permute-done((bf16[3,4,72,512]{3,2,1,0:T(8,128)(2,1)}, bf16[3,4,72,512]{3,2,1,0:T(8,128)(2,1)}, u32[]{:S(2)}, u32[]{:S(2)}) %collective-permute-start.2) | collective-permute-done | bytes 884768 | tf_op jit(solution)/shard_map/ppermute | solution.py:202
  57.1 1.3 select_select_fusion.b_ref
  58.5 10.9 %attend.1 = (bf16[4,72,512]{2,1,0:T(8,128)(2,1)S(1)}, bf16[4,72,512]{2,1,0:T(8,128)(2,1)S(1)}, f32[4,1,512]{2,1,0:T(1,128)S(1)}, f32[4,1,512]{2,1,0:T(1,128)S(1)}, f32[4,72,128]{2,1,0:T(8,128)S(1)}) custom-call(f32[1]{0:T(128)} %bitcast.3.far_ref, bf16[3,4,72,512]{3,2,1,0:T(8,128)(2,1)S(1)} %get-tuple-element.38.a_ref, ...), custom_call_target="tpu_custom_call" | custom-call | flops 1207959552 | bytes 5000000 | tf_op jit(solution)/shard_map/attend/pallas_call | solution.py:115
  75.6 1.3 collective-permute-start.8
  76.9 5.0 %collective-permute-start.7 = (f32[2,2,288]{2,1,0:T(2,128)S(1)}, f32[2,2,288]{2,1,0:T(2,128)S(1)}, u32[]{:S(2)}, u32[]{:S(2)}) collective-permute-start(f32[2,2,288]{2,1,0:T(2,128)S(1)} %fusion.11), channel_id=1, source_target_pairs={{0,2},{1,3},{2,4},{3,5},{4,6},{5,7},{6,8},{7,9},{8,10},{9,11},{10,... | collective-permute-start | bytes 13832 | tf_op jit(solution)/shard_map/ppermute | solution.py:239
  84.7 1.2 fusion.9
  92.5 14.2 %grads.1 = (bf16[3,4,72,512]{3,2,1,0:T(8,128)(2,1)S(1)}, bf16[3,4,72,512]{3,2,1,0:T(8,128)(2,1)S(1)}) custom-call(f32[1]{0:T(128)} %bitcast.3.far_ref, bf16[3,4,72,512]{3,2,1,0:T(8,128)(2,1)S(1)} %get-tuple-element.38.a_ref, bf16[3,4,72,512]{3,2,1,0:T(8,128)(2,1)S(1)} %select_select_fusion.b_ref, bf16[4,72,512]{2,1,0:T(8,128)(2,1)S(1)} %copy-done, ...), custom_call_target="tpu_custom_call" | custom-call | flops 3019898880 | bytes 8000000 | tf_op jit(solution)/shard_map/grads/pallas_call | solution.py:146
  106.6 3.0 %collective-permute-start.9 = (bf16[3,4,72,512]{3,2,1,0:T(8,128)(2,1)S(1)}, bf16[3,4,72,512]{3,2,1,0:T(8,128)(2,1)S(1)}, u32[]{:S(2)}, u32[]{:S(2)}) collective-permute-start(bf16[3,4,72,512]{3,2,1,0:T(8,128)(2,1)S(1)} %get-tuple-element.16), channel_id=1, source_target_pairs={{0,2},{1,3},{2,0},{3,1},{4,6},{5,7},{6,4},{7,5},{8,10},{9,11},{10,... | collective-permute-start | bytes 2654216 | tf_op jit(solution)/shard_map/ppermute | solution.py:197
  109.6 19.2 %collective-permute-done.9 = bf16[3,4,72,512]{3,2,1,0:T(8,128)(2,1)S(1)} collective-permute-done((bf16[3,4,72,512]{3,2,1,0:T(8,128)(2,1)S(1)}, bf16[3,4,72,512]{3,2,1,0:T(8,128)(2,1)S(1)}, u32[]{:S(2)}, u32[]{:S(2)}) %collective-permute-start.9) | collective-permute-done | bytes 884768 | tf_op jit(solution)/shard_map/ppermute | solution.py:197
  128.8 5.1 %collective-permute-start.10 = (bf16[3,4,72,512]{3,2,1,0:T(8,128)(2,1)S(1)}, bf16[3,4,72,512]{3,2,1,0:T(8,128)(2,1)S(1)}, u32[]{:S(2)}, u32[]{:S(2)}) collective-permute-start(bf16[3,4,72,512]{3,2,1,0:T(8,128)(2,1)S(1)} %collective-permute-done.9), channel_id=1, source_target_pairs={{0,4},{1,5},{4,8},{5,9},{6,2},{7,3},{8,12},{9,13},{10,6},{11,7},{1... | collective-permute-start | bytes 2654216 | tf_op jit(solution)/shard_map/ppermute | solution.py:202
  133.9 17.1 %collective-permute-done.10 = bf16[3,4,72,512]{3,2,1,0:T(8,128)(2,1)S(1)} collective-permute-done((bf16[3,4,72,512]{3,2,1,0:T(8,128)(2,1)S(1)}, bf16[3,4,72,512]{3,2,1,0:T(8,128)(2,1)S(1)}, u32[]{:S(2)}, u32[]{:S(2)}) %collective-permute-start.10) | collective-permute-done | bytes 884768 | tf_op jit(solution)/shard_map/ppermute | solution.py:202
  152.0 1.3 select_bitcast_fusion.3
  153.5 1.2 and_select_fusion
  154.7 32.5 %psum.7 = f32[6]{0:T(128)} all-reduce(f32[6]{0:T(128)S(1)} %and_select_fusion), channel_id=1, replica_groups=mesh['groups'=2,'ctx'=16] {'ctx'}, use_global_device_ids=true, to_apply=%region_8.9 | all-reduce | flops 6 | bytes 48 | tf_op jit(solution)/shard_map/psum | solution.py:248
  187.7 1.1 copy.33
  188.8 1.1 copy.32
  189.9 1.1 copy.31
  (102 shorter events, 20.4 us)
Async XLA Ops:
  0.6 2.7 %copy-start.8 = (bf16[256,1152]{1,0:T(8,128)(2,1)S(1)}, bf16[256,1152]{1,0:T(8,128)(2,1)}, u32[]{:S(2)}) copy-start(bf16[256,1152]{1,0:T(8,128)(2,1)} %param.11) | copy-start | bytes 1769476
  3.9 5.8 %collective-permute-start = (bf16[3,2,4,72,256]{4,3,2,0,1:T(8,128)(2,1)S(1)}, bf16[3,2,4,72,256]{4,3,2,0,1:T(8,128)(2,1)S(1)}, u32[]{:S(2)}, u32[]{:S(2)}) collective-permute-start(bf16[3,2,4,72,256]{4,3,2,0,1:T(8,128)(2,1)S(1)} %pad_maximum_fusion.2), channel_id=1, source_target_pairs={{0,1},{1,0},{2,3},{3,2},{4,5},{5,4},{6,7},{7,6},{8,9},{9,8},{10,11... | collective-permute-start | bytes 2654216 | tf_op jit(solution)/shard_map/ppermute | solution.py:194
  9.8 27.9 %copy-start.9 = (bf16[256,1152]{1,0:T(8,128)(2,1)S(1)}, bf16[256,1152]{1,0:T(8,128)(2,1)}, u32[]{:S(2)}) copy-start(bf16[256,1152]{1,0:T(8,128)(2,1)} %param.12) | copy-start | bytes 1769476
  10.0 29.3 %copy-start.10 = (f32[6,1152]{1,0:T(8,128)S(1)}, f32[6,1152]{1,0:T(8,128)}, u32[]{:S(2)}) copy-start(f32[6,1152]{1,0:T(8,128)} %param.16) | copy-start | bytes 82948
  10.0 23.0 %collective-permute-start.1 = (bf16[3,4,72,512]{3,2,1,0:T(8,128)(2,1)S(1)}, bf16[3,4,72,512]{3,2,1,0:T(8,128)(2,1)}, u32[]{:S(2)}, u32[]{:S(2)}) collective-permute-start(bf16[3,4,72,512]{3,2,1,0:T(8,128)(2,1)S(1)} %get-tuple-element.37), channel_id=1, source_target_pairs={{0,2},{1,3},{2,0},{3,1},{4,6},{5,7},{6,4},{7,5},{8,10},{9,11},{10,... | collective-permute-start | bytes 2654216 | tf_op jit(solution)/shard_map/ppermute | solution.py:197
  33.0 24.1 %collective-permute-start.2 = (bf16[3,4,72,512]{3,2,1,0:T(8,128)(2,1)}, bf16[3,4,72,512]{3,2,1,0:T(8,128)(2,1)}, u32[]{:S(2)}, u32[]{:S(2)}) collective-permute-start(bf16[3,4,72,512]{3,2,1,0:T(8,128)(2,1)} %collective-permute-done.1), channel_id=1, source_target_pairs={{0,4},{1,5},{4,8},{5,9},{6,2},{7,3},{8,12},{9,13},{10,6},{11,7},{1... | collective-permute-start | bytes 2654216 | tf_op jit(solution)/shard_map/ppermute | solution.py:202
  38.0 1.6 collective-permute-start.3
  40.4 9.2 %collective-permute-start.4 = (bf16[1,4,72,512]{3,2,1,0:T(8,128)(2,1)S(1)}, bf16[1,4,72,512]{3,2,1,0:T(8,128)(2,1)S(1)}, u32[]{:S(2)}, u32[]{:S(2)}) collective-permute-start(bf16[1,4,72,512]{3,2,1,0:T(8,128)(2,1)S(1)} %get-tuple-element.39), channel_id=1, source_target_pairs={{0,2},{1,3},{2,0},{3,1},{4,6},{5,7},{6,4},{7,5},{8,10},{9,11},{10,... | collective-permute-start | bytes 884744 | tf_op jit(solution)/shard_map/ppermute | solution.py:197
  49.6 32.2 %collective-permute-start.5 = (bf16[1,4,72,512]{3,2,1,0:T(8,128)(2,1)S(1)}, bf16[1,4,72,512]{3,2,1,0:T(8,128)(2,1)S(1)}, u32[]{:S(2)}, u32[]{:S(2)}) collective-permute-start(bf16[1,4,72,512]{3,2,1,0:T(8,128)(2,1)S(1)} %collective-permute-done.4), channel_id=1, source_target_pairs={{0,4},{1,5},{4,8},{5,9},{6,2},{7,3},{8,12},{9,13},{10,6},{11,7},{1... | collective-permute-start | bytes 884744 | tf_op jit(solution)/shard_map/ppermute | solution.py:202
  58.4 12.5 %copy-start.15 = (pred[2]{0:T(512)(128)(4,1)S(1)}, pred[2]{0:T(512)(128)(4,1)}, u32[]{:S(2)}) copy-start(pred[2]{0:T(512)(128)(4,1)} %iota_compare_fusion) | copy-start | bytes 10
  58.4 12.6 %copy-start.12 = (pred[2]{0:T(512)(128)(4,1)S(1)}, pred[2]{0:T(512)(128)(4,1)}, u32[]{:S(2)}) copy-start(pred[2]{0:T(512)(128)(4,1)} %iota_compare_fusion.1) | copy-start | bytes 10
  58.4 12.7 %copy-start.14 = (f32[2]{0:T(128)S(1)}, f32[2]{0:T(128)}, u32[]{:S(2)}) copy-start(f32[2]{0:T(128)} %param.17) | copy-start | bytes 28
  58.4 13.3 %copy-start.17 = (s32[6]{0:T(128)S(1)}, s32[6]{0:T(128)}, u32[]{:S(2)}) copy-start(s32[6]{0:T(128)} %param.14) | copy-start | bytes 76
  58.5 13.9 %copy-start.18 = (s32[6]{0:T(128)S(1)}, s32[6]{0:T(128)}, u32[]{:S(2)}) copy-start(s32[6]{0:T(128)} %param.15) | copy-start | bytes 76
  58.5 26.0 %copy-start.11 = (f32[6,1152]{1,0:T(8,128)S(1)}, f32[6,1152]{1,0:T(8,128)}, u32[]{:S(2)}) copy-start(f32[6,1152]{1,0:T(8,128)} %param.16) | copy-start | bytes 82948
  58.5 26.0 %copy-start.13 = (f32[6]{0:T(128)S(1)}, f32[6]{0:T(128)}, u32[]{:S(2)}) copy-start(f32[6]{0:T(128)} %add_sqrt_fusion) | copy-start | bytes 76
  71.1 4.4 %collective-permute-start.6 = (f32[2,2,288]{2,1,0:T(2,128)S(1)}, f32[2,2,288]{2,1,0:T(2,128)S(1)}, u32[]{:S(2)}, u32[]{:S(2)}) collective-permute-start(f32[2,2,288]{2,1,0:T(2,128)S(1)} %broadcast_select_fusion.3), channel_id=1, source_target_pairs={{0,1},{1,0},{2,3},{3,2},{4,5},{5,4},{6,7},{7,6},{8,9},{9,8},{10,11... | collective-permute-start | bytes 13832 | tf_op jit(solution)/shard_map/ppermute | solution.py:194
  75.6 7.0 %collective-permute-start.8 = (f32[2,2,288]{2,1,0:T(2,128)S(1)}, f32[2,2,288]{2,1,0:T(2,128)S(1)}, u32[]{:S(2)}, u32[]{:S(2)}) collective-permute-start(f32[2,2,288]{2,1,0:T(2,128)S(1)} %fusion.11), channel_id=1, source_target_pairs={{2,0},{3,1},{4,2},{5,3},{6,4},{7,5},{8,6},{9,7},{10,8},{11,9},{12,... | collective-permute-start | bytes 13832 | tf_op jit(solution)/shard_map/ppermute | solution.py:240
  76.9 6.3 %collective-permute-start.7 = (f32[2,2,288]{2,1,0:T(2,128)S(1)}, f32[2,2,288]{2,1,0:T(2,128)S(1)}, u32[]{:S(2)}, u32[]{:S(2)}) collective-permute-start(f32[2,2,288]{2,1,0:T(2,128)S(1)} %fusion.11), channel_id=1, source_target_pairs={{0,2},{1,3},{2,4},{3,5},{4,6},{5,7},{6,8},{7,9},{8,10},{9,11},{10,... | collective-permute-start | bytes 13832 | tf_op jit(solution)/shard_map/ppermute | solution.py:239
  106.6 22.2 %collective-permute-start.9 = (bf16[3,4,72,512]{3,2,1,0:T(8,128)(2,1)S(1)}, bf16[3,4,72,512]{3,2,1,0:T(8,128)(2,1)S(1)}, u32[]{:S(2)}, u32[]{:S(2)}) collective-permute-start(bf16[3,4,72,512]{3,2,1,0:T(8,128)(2,1)S(1)} %get-tuple-element.16), channel_id=1, source_target_pairs={{0,2},{1,3},{2,0},{3,1},{4,6},{5,7},{6,4},{7,5},{8,10},{9,11},{10,... | collective-permute-start | bytes 2654216 | tf_op jit(solution)/shard_map/ppermute | solution.py:197
  128.8 22.2 %copy-start.6 = (bf16[3,4,72,512]{3,2,1,0:T(8,128)(2,1)}, bf16[3,4,72,512]{3,2,1,0:T(8,128)(2,1)S(1)}, u32[]{:S(2)}) copy-start(bf16[3,4,72,512]{3,2,1,0:T(8,128)(2,1)S(1)} %collective-permute-done.9) | copy-start | bytes 2654212
  128.8 22.2 %collective-permute-start.10 = (bf16[3,4,72,512]{3,2,1,0:T(8,128)(2,1)S(1)}, bf16[3,4,72,512]{3,2,1,0:T(8,128)(2,1)S(1)}, u32[]{:S(2)}, u32[]{:S(2)}) collective-permute-start(bf16[3,4,72,512]{3,2,1,0:T(8,128)(2,1)S(1)} %collective-permute-done.9), channel_id=1, source_target_pairs={{0,4},{1,5},{4,8},{5,9},{6,2},{7,3},{8,12},{9,13},{10,6},{11,7},{1... | collective-permute-start | bytes 2654216 | tf_op jit(solution)/shard_map/ppermute | solution.py:202
  151.0 1.0 copy-start.7
  153.4 33.8 %collective-permute-start.11 = (bf16[2,3,4,72,256]{4,3,2,1,0:T(8,128)(2,1)S(1)}, bf16[2,3,4,72,256]{4,3,2,1,0:T(8,128)(2,1)S(1)}, u32[]{:S(2)}, u32[]{:S(2)}) collective-permute-start(bf16[2,3,4,72,256]{4,3,2,1,0:T(8,128)(2,1)S(1)} %pad_maximum_fusion.1), channel_id=1, source_target_pairs={{0,1},{1,0},{2,3},{3,2},{4,5},{5,4},{6,7},{7,6},{8,9},{9,8},{10,11... | collective-permute-start | bytes 2654216 | tf_op jit(solution)/shard_map/ppermute | solution.py:194
  (7 other events, 6.0 us)

commit v2 on v0

v2 whole, which is shorter than its diff:
```python
import jax
import jax.numpy as jnp
from jax import lax
from jax.experimental import pallas as pl
from jax.experimental.pallas import tpu as pltpu
from jax.sharding import PartitionSpec as P

HEADS = 16
HEAD_DIM = 72
BLOCK = 512
QUARTER = 4
CHUNK = 256
TEMPER = 10.0
LOSS_SCALE = 65536.0
EPSILON = 1e-06
SCALE = HEAD_DIM ** (-0.5)
LOG2E = 1.4426950408889634
FAR = -1e30


def dot_over(x, y, dim_x, dim_y):
    return lax.dot_general(
        x, y, (((dim_x,), (dim_y,)), ((), ())), preferred_element_type=jnp.float32
    )


def neighbours():
    devices = lax.axis_size("ctx")
    me = lax.axis_index("ctx")
    odd = (me // 2) % 2
    across = me + 2 - 4 * odd
    target = me + 4 - 8 * odd
    source = me - 4 + 8 * odd
    has_target = (target >= 0) & (target < devices)
    has_source = (source >= 0) & (source < devices)
    return across, target, source, has_target, has_source


def signal(barrier, device):
    pl.semaphore_signal(
        barrier, inc=1, device_id={"ctx": device}, device_id_type=pl.DeviceIdType.MESH
    )


def greet():
    across, target, source, has_target, has_source = neighbours()
    barrier = pltpu.get_barrier_semaphore()
    signal(barrier, across)
    pl.when(has_target)(lambda: signal(barrier, target))
    pl.when(has_source)(lambda: signal(barrier, source))
    peers = 1 + has_target.astype(jnp.int32) + has_source.astype(jnp.int32)
    pl.semaphore_wait(barrier, peers)


def hop(src, dst, sems, h, device):
    return pltpu.make_async_remote_copy(
        src_ref=src.at[h],
        dst_ref=dst.at[h],
        send_sem=sems.at[0, h],
        recv_sem=sems.at[1, h],
        device_id={"ctx": device},
        device_id_type=pl.DeviceIdType.MESH,
    )


def chosen(flag, x, y):
    return jnp.where(flag, x.astype(jnp.float32), y.astype(jnp.float32)).astype(jnp.bfloat16)


def attend_kernel(
    far_ref, flag_ref, a_ref, given_ref, b_ref, att_ref, lse_ref, pool_ref,
    near_ref, relay_ref, near_sems, relay_sems,
):
    across, target, _, has_target, has_source = neighbours()

    @pl.when(jnp.logical_not(has_source))
    def _():
        relay_ref[...] = jnp.zeros_like(relay_ref)

    greet()
    for h in range(QUARTER):
        hop(given_ref, near_ref, near_sems, h, across).start()

    def pass_on(h):
        hop(given_ref, near_ref, near_sems, h, across).wait_recv()
        pl.when(has_target)(lambda: hop(near_ref, relay_ref, relay_sems, h, target).start())

    pass_on(0)
    far = far_ref[0]
    paired = flag_ref[0] == 1
    beside = flag_ref[1] == 1
    lane = lax.broadcasted_iota(jnp.int32, (HEAD_DIM, 128), 1)

    def one_head(h, gathered):
        pl.when(h < QUARTER - 1)(lambda: pass_on(h + 1))
        pl.when(has_source)(
            lambda: hop(near_ref, relay_ref, relay_sems, h, target).wait_recv()
        )
        for kind in range(4):
            b_ref[h, kind] = chosen(
                paired,
                chosen(beside, near_ref[h, kind], relay_ref[h, kind]),
                given_ref[h, kind],
            )
        sides = (a_ref, b_ref)
        for own in range(2):
            pool = jnp.zeros((HEAD_DIM, 1), jnp.float32)
            for start in range(0, BLOCK, CHUNK):
                q = sides[own][h, 0, :, start : start + CHUNK]
                scores = []
                for side in range(2):
                    s = dot_over(sides[side][h, 1], q, 0, 0) * (SCALE * LOG2E)
                    scores.append(s if side == own else s + far)
                top = jnp.maximum(
                    jnp.max(scores[0], axis=0, keepdims=True),
                    jnp.max(scores[1], axis=0, keepdims=True),
                )
                parts = [jnp.exp2(s - top) for s in scores]
                total = jnp.sum(parts[0], axis=0, keepdims=True) + jnp.sum(
                    parts[1], axis=0, keepdims=True
                )
                scale = 1.0 / total
                att = jnp.zeros((HEAD_DIM, CHUNK), jnp.float32)
                for side in range(2):
                    probs = (parts[side] * scale).astype(jnp.bfloat16)
                    att = att + dot_over(sides[side][h, 2], probs, 1, 0)
                att = att.astype(jnp.bfloat16)
                att_ref[own, h, :, start : start + CHUNK] = att
                lse_ref[own, h, :, start : start + CHUNK] = top + jnp.log2(total)
                pool = pool + jnp.sum(att.astype(jnp.float32), axis=1, keepdims=True)
            gathered = jnp.where(lane == own * QUARTER + h, pool, gathered)
        return gathered

    pool_ref[...] = lax.fori_loop(
        0, QUARTER, one_head, jnp.zeros((HEAD_DIM, 128), jnp.float32)
    )
    for h in range(QUARTER):
        hop(given_ref, near_ref, near_sems, h, across).wait_send()

        @pl.when(has_target)
        def _():
            hop(near_ref, relay_ref, relay_sems, h, target).wait_send()


def grads_kernel(
    far_ref, flag_ref, a_ref, b_ref, att_ref, lse_ref, extra_ref, whole_ref,
    out_ref, near_ref, relay_ref, acc_ref, near_sems, relay_sems,
):
    across, target, _, has_target, has_source = neighbours()

    @pl.when(jnp.logical_not(has_source))
    def _():
        relay_ref[...] = jnp.zeros_like(relay_ref)

    greet()
    far = far_ref[0]
    paired = flag_ref[0] == 1
    beside = flag_ref[1] == 1
    late = flag_ref[2] == 1
    given_ref = out_ref.at[1]

    def pass_on(h):
        hop(given_ref, near_ref, near_sems, h, across).wait_recv()
        pl.when(has_target)(lambda: hop(near_ref, relay_ref, relay_sems, h, target).start())

    def one_head(h, carry):
        sides = (a_ref, b_ref)
        first = True
        for own in range(2):
            for start in range(0, BLOCK, CHUNK):
                span = slice(start, start + CHUNK)
                q = sides[own][h, 0, :, span]
                up = sides[own][h, 3, :, span].astype(jnp.float32)
                grad = (up + extra_ref[own, h]).astype(jnp.bfloat16)
                att = att_ref[own, h, :, span].astype(jnp.float32)
                lse = lse_ref[own, h, :, span]
                delta = jnp.sum(grad.astype(jnp.float32) * att, axis=0, keepdims=True)
                grad_q = jnp.zeros((HEAD_DIM, CHUNK), jnp.float32)
                for side in range(2):
                    k = sides[side][h, 1]
                    s = dot_over(k, q, 0, 0) * (SCALE * LOG2E)
                    if side != own:
                        s = s + far
                    probs = jnp.exp2(s - lse)
                    grad_probs = dot_over(sides[side][h, 2], grad, 0, 0)
                    grad_scores = (probs * (grad_probs - delta)).astype(jnp.bfloat16)
                    grad_q = grad_q + dot_over(k, grad_scores, 1, 0)
                    grad_k = dot_over(q, grad_scores, 1, 1)
                    grad_v = dot_over(grad, probs.astype(jnp.bfloat16), 1, 1)
                    if first:
                        acc_ref[side, 0] = grad_k
                        acc_ref[side, 1] = grad_v
                    else:
                        acc_ref[side, 0] += grad_k
                        acc_ref[side, 1] += grad_v
                first = False
                out_ref[own, h, 0, :, span] = (grad_q * SCALE).astype(jnp.bfloat16)
        for side in range(2):
            out_ref[side, h, 1] = (acc_ref[side, 0] * SCALE).astype(jnp.bfloat16)
            out_ref[side, h, 2] = acc_ref[side, 1].astype(jnp.bfloat16)
        hop(given_ref, near_ref, near_sems, h, across).start()
        pl.when(h > 0)(lambda: pass_on(h - 1))
        return carry

    lax.fori_loop(0, QUARTER, one_head, 0)
    pass_on(QUARTER - 1)

    def settle(h, carry):
        pl.when(has_source)(
            lambda: hop(near_ref, relay_ref, relay_sems, h, target).wait_recv()
        )
        for kind in range(3):
            mine, other = out_ref[0, h, kind], out_ref[1, h, kind]
            back = chosen(beside, near_ref[h, kind], relay_ref[h, kind])
            other = chosen(paired, back, other)
            whole_ref[0, h, kind] = chosen(late, other, mine)
            whole_ref[1, h, kind] = chosen(late, mine, other)
        return carry

    lax.fori_loop(0, QUARTER, settle, 0)
    for h in range(QUARTER):
        hop(given_ref, near_ref, near_sems, h, across).wait_send()

        @pl.when(has_target)
        def _():
            hop(near_ref, relay_ref, relay_sems, h, target).wait_send()


def gather_kernel(x_ref, out_ref, send_sem, recv_sem):
    devices = lax.axis_size("ctx")
    me = lax.axis_index("ctx")
    barrier = pltpu.get_barrier_semaphore()

    def peer(step):
        return (me + step) % devices

    def greet_one(step, carry):
        signal(barrier, peer(step))
        return carry

    lax.fori_loop(1, devices, greet_one, 0)
    pl.semaphore_wait(barrier, devices - 1)

    def copy(step, slot):
        return pltpu.make_async_remote_copy(
            src_ref=x_ref,
            dst_ref=out_ref.at[slot],
            send_sem=send_sem.at[step],
            recv_sem=recv_sem.at[step],
            device_id={"ctx": peer(step)},
            device_id_type=pl.DeviceIdType.MESH,
        )

    def send_one(step, carry):
        copy(step, me).start()
        return carry

    def wait_one(step, carry):
        done = copy(step, (me + devices - step) % devices)
        done.wait_recv()
        done.wait_send()
        return carry

    lax.fori_loop(1, devices, send_one, 0)
    out_ref[me] = x_ref[...]
    lax.fori_loop(1, devices, wait_one, 0)


SMEM = pl.BlockSpec(memory_space=pltpu.SMEM)
VMEM = pl.BlockSpec(memory_space=pltpu.VMEM)


def params(number):
    return pltpu.CompilerParams(
        vmem_limit_bytes=48 * 2**20, collective_id=number, has_side_effects=True
    )


def attend(far, flags, a, given):
    tiles = (QUARTER, 4, HEAD_DIM, BLOCK)
    sems = pltpu.SemaphoreType.DMA((2, QUARTER))
    return pl.pallas_call(
        attend_kernel,
        in_specs=[SMEM, SMEM, VMEM, VMEM],
        out_specs=[VMEM] * 4,
        out_shape=[
            jax.ShapeDtypeStruct(tiles, jnp.bfloat16),
            jax.ShapeDtypeStruct((2, QUARTER, HEAD_DIM, BLOCK), jnp.bfloat16),
            jax.ShapeDtypeStruct((2, QUARTER, 1, BLOCK), jnp.float32),
            jax.ShapeDtypeStruct((HEAD_DIM, 128), jnp.float32),
        ],
        scratch_shapes=[
            pltpu.VMEM(tiles, jnp.bfloat16), pltpu.VMEM(tiles, jnp.bfloat16), sems, sems,
        ],
        compiler_params=params(0),
        name="attend",
    )(far, flags, a, given)


def grads(far, flags, a, b, att, lse, extra):
    tiles = (QUARTER, 3, HEAD_DIM, BLOCK)
    sems = pltpu.SemaphoreType.DMA((2, QUARTER))
    return pl.pallas_call(
        grads_kernel,
        in_specs=[SMEM, SMEM] + [VMEM] * 5,
        out_specs=VMEM,
        out_shape=jax.ShapeDtypeStruct((2,) + tiles, jnp.bfloat16),
        scratch_shapes=[
            pltpu.VMEM((2,) + tiles, jnp.bfloat16),
            pltpu.VMEM(tiles, jnp.bfloat16),
            pltpu.VMEM(tiles, jnp.bfloat16),
            pltpu.VMEM((2, 2, HEAD_DIM, BLOCK), jnp.float32),
            sems, sems,
        ],
        compiler_params=params(1),
        name="grads",
    )(far, flags, a, b, att, lse, extra)


def gather(x):
    devices = lax.axis_size("ctx")
    return pl.pallas_call(
        gather_kernel,
        in_specs=[VMEM],
        out_specs=VMEM,
        out_shape=jax.ShapeDtypeStruct((devices,) + x.shape, x.dtype),
        scratch_shapes=[
            pltpu.SemaphoreType.DMA((devices,)), pltpu.SemaphoreType.DMA((devices,)),
        ],
        compiler_params=params(2),
        name="gather",
    )(x)


def contrast(pooled_sum, lengths, modality, pairs, texts, modality_bias):
    count_rows = lengths.shape[0]
    sizes = (lengths * BLOCK).astype(jnp.float32)
    pooled = pooled_sum / sizes[:, None]
    norm = jnp.sqrt(jnp.sum(pooled * pooled, axis=1, keepdims=True) + EPSILON)
    unit = pooled / norm
    text_unit = texts / jnp.sqrt(jnp.sum(texts * texts, axis=1, keepdims=True) + EPSILON)
    bias = jnp.where(modality == 0, modality_bias[0], modality_bias[1])
    logits = TEMPER * jnp.dot(unit, text_unit.T, precision=lax.Precision.HIGHEST) + bias[:, None]
    labels = jnp.where(
        pairs[:, None] == jnp.arange(count_rows, dtype=jnp.int32)[None, :], 1.0, -1.0
    )
    margin = labels * logits
    loss = jnp.sum(jax.nn.softplus(-margin), axis=1)
    grad_logits = -labels * jax.nn.sigmoid(-margin) * (LOSS_SCALE / count_rows)
    grad_unit = TEMPER * jnp.dot(grad_logits, text_unit, precision=lax.Precision.HIGHEST)
    grad_pooled = (grad_unit - unit * jnp.sum(unit * grad_unit, axis=1, keepdims=True)) / norm
    return (loss, grad_pooled / sizes[:, None])


def on_device(queries, keys, values, upstream, lengths, modality, pairs, texts, modality_bias):
    rows = queries.shape[0]
    devices = lax.axis_size("ctx")
    count = lengths.shape[0]
    blocks = devices // 2
    place = lax.axis_index("ctx")
    block, core = place // 2, place % 2
    ends = jnp.cumsum(lengths)
    every = jnp.arange(blocks, dtype=jnp.int32)
    scenes = jnp.sum((every[:, None] >= ends[None, :]).astype(jnp.int32), axis=1)
    lengths_at = lengths[scenes]
    paired_at = lengths_at == 2
    seconds = every - (ends[scenes] - lengths_at)
    scene, second, paired = scenes[block], seconds[block], paired_at[block]
    beside = (block + 1 - 2 * second) == (block ^ 1)
    far = jnp.where(paired, 0.0, FAR).astype(jnp.float32).reshape(1)
    flags = jnp.stack([paired, beside, second == 1]).astype(jnp.int32)

    def swap_core(x):
        return lax.ppermute(x, "ctx", [(i, i ^ 1) for i in range(devices)])

    split = jnp.stack(
        [
            x.T.reshape(2, 2, QUARTER, HEAD_DIM, rows)
            for x in (queries, keys, values, upstream)
        ],
        axis=3,
    )
    mine = lax.dynamic_index_in_dim(split, core, 1, keepdims=False)
    theirs = swap_core(lax.dynamic_index_in_dim(split, 1 - core, 1, keepdims=False))
    whole = jnp.concatenate([mine, theirs], axis=-1)
    a = lax.dynamic_index_in_dim(whole, second, 0, keepdims=False)
    given = lax.dynamic_index_in_dim(whole, 1 - second, 0, keepdims=False)
    b, att, lse, pool = attend(far, flags, a, given)

    message = jnp.pad(pool[:, : 2 * QUARTER].T, ((0, 0), (0, 128 - HEAD_DIM)))
    pools = gather(message)[:, :, :HEAD_DIM].reshape(blocks, 2, 2, QUARTER * HEAD_DIM)
    both = pools[:, :, 0] + pools[:, :, 1]
    halves = []
    for half in range(2):
        shared = jnp.where((seconds == half)[:, None, None], both, 0.0)
        halves.append(jnp.where(paired_at[:, None, None], shared, pools[:, :, half]))
    sums = jnp.stack(halves, axis=1).reshape(blocks, HEADS * HEAD_DIM)
    member = scenes[None, :] == jnp.arange(count, dtype=jnp.int32)[:, None]
    pooled_sum = jnp.sum(jnp.where(member[:, :, None], sums[None], 0.0), axis=1)
    loss, per_token = contrast(pooled_sum, lengths, modality, pairs, texts, modality_bias)
    per_half = lax.dynamic_index_in_dim(
        per_token[scene].reshape(2, 2, QUARTER, HEAD_DIM, 1), core, 1, keepdims=False
    )
    own = per_half[second]
    extra = jnp.stack([own, jnp.where(paired, own, per_half[1])])
    whole = grads(far, flags, a, b, att, lse, extra)
    theirs = swap_core(whole[..., rows:])
    mine = whole[..., :rows]
    even = jnp.where(core == 0, mine, theirs)
    odd = jnp.where(core == 0, theirs, mine)
    done = jnp.stack([even, odd], axis=1)
    done = done.transpose(3, 5, 0, 1, 2, 4).reshape(3, rows, HEADS * HEAD_DIM)
    return done[0], done[1], done[2], loss


def solution(mesh):
    tokens = P(("groups", "ctx"), None)
    in_specs = (
        tokens, tokens, tokens, tokens,
        P("groups"), P("groups"), P("groups"), P("groups", None), P(),
    )
    out_specs = (tokens, tokens, tokens, P("groups"))
    return jax.shard_map(
        on_device, mesh=mesh, in_specs=in_specs, out_specs=out_specs, check_vma=False
    )
```

time: 499 us -> 118 us (0.24)
  waiting for transfers between devices: 185 us -> 2.19 us
  starting transfers between devices: 82.4 us -> 2.79 us
  Pallas kernels: 0 us -> 77 us
  matrix products: 78.1 us -> 1.19 us
  blocking collectives: 50.9 us -> 0 us
  local copies, waits for them, and re-layouts: 68.3 us -> 17.6 us
  other arithmetic: 26.8 us -> 8.12 us
  between operations: 2.16 us -> 8.13 us
    ppermute x18 -> x2, waiting for transfers between devices: 185 us -> 2.19 us  [swap_core(): return lax.ppermute(x, 'ctx', [(i, i ^ 1) for i in range(devices)])]
    ppermute x18 -> x2, starting transfers between devices: 82.4 us -> 2.79 us  [swap_core(): return lax.ppermute(x, 'ctx', [(i, i ^ 1) for i in range(devices)])]
    pallas_call x0 -> x3, Pallas kernels: none -> 77 us  [the longest x1 39 us: attend(): pl.pallas_call(attend_kernel, in_specs=[SMEM, SMEM, VMEM, VMEM], out_spec...]
    dot_general x43 -> x0, matrix products: 76.9 us -> none  [the longest x7 18.5 us: tile_grads(): jnp.einsum('hqk,hqd->hkd', probs.astype(jnp.bfloat16), grad_heads, prefer...]
    psum x1 -> x0, blocking collectives: 50.9 us -> none  [on_device(): pooled_sum = lax.psum(partial_sums, 'ctx')]
    reshape x14 -> x1, local copies, waits for them, and re-layouts: 36.4 us -> 0.12 us  [on_device(): gather(message)[:, :, :HEAD_DIM].reshape(blocks, 2, 2, QUARTER * HEAD_DIM)]
    slice x18 -> x6, local copies, waits for them, and re-layouts: 20.6 us -> 0.34 us  [the longest x4 0.24 us: on_device(): return (done[0], done[1], done[2], loss)]
    convert_element_type x3 -> x1, other arithmetic: 10.4 us -> 0.72 us  [on_device(): flags = jnp.stack([paired, beside, second == 1]).astype(jnp.int32)]
  transfers between devices with their start and end apart: 18 -> 2, of which waited for: 7 -> 1; matrix products, arithmetic and copies ran while one was open for 15% -> 5% of each run, Pallas kernels for 0% -> 0%
where the time goes in v2:
time: 118 us; the launch traced here: 117 us
  Pallas kernels  77 us (65%)
  local copies, waits for them, and re-layouts  17.6 us (15%)
  between operations  8.13 us (7%)
  other arithmetic  8.12 us (7%)
  starting transfers between devices  2.79 us (2%)
  waiting for transfers between devices  2.19 us (2%)
  matrix products  1.19 us (1%)
    pallas_call x1, Pallas kernels, attend(): pl.pallas_call(attend_kernel, in_specs=[SMEM, SMEM, VMEM, VMEM], out_spec...  39 us
    pallas_call x1, Pallas kernels, grads(): pl.pallas_call(grads_kernel, in_specs=[SMEM, SMEM] + [VMEM] * 5, out_spec...  29.9 us
    unnamed x29, local copies, waits for them, and re-layouts  10.5 us
    pallas_call x1, Pallas kernels, gather(): pl.pallas_call(gather_kernel, in_specs=[VMEM], out_specs=VMEM, out_shape=...  8.05 us
    ppermute x2, starting transfers between devices, swap_core(): return lax.ppermute(x, 'ctx', [(i, i ^ 1) for i in range(devices)])  2.79 us
  transfers between devices with their start and end apart: 2, of which 1 were waited for; matrix products, arithmetic and copies ran while one was open for 5% of the time, Pallas kernels for 0%

profile of v2, /device:TPU:25, one launch (start us, length us, event | category | flops | bytes accessed | tf_op | source)
XLA Modules:
  0.0 117.0 jit_solution(12061150333574161823)
XLA Ops:
  0.7 1.4 %copy.66 = bf16[256,1152]{0,1:T(8,128)(2,1)S(1)} copy(bf16[256,1152]{1,0:T(8,128)(2,1)} %param.9) | data formatting | bytes 1179648 | tf_op args[0]
  2.1 1.3 %copy.67 = bf16[256,1152]{0,1:T(8,128)(2,1)S(1)} copy(bf16[256,1152]{1,0:T(8,128)(2,1)} %param.10) | data formatting | bytes 1179648 | tf_op args[1]
  4.4 1.1 copy.100
  5.5 0.7 collective-permute-start
  7.1 0.6 gather_fusion
  16.8 0.7 add_convert_fusion.flag_ref
  18.3 1.3 %compare_select_fusion.2 = (f32[6]{0:T(128)S(1)}, f32[6]{0:T(128)S(1)}) fusion(s32[6]{0:T(128)S(1)} %copy-done.9, f32[]{:T(128)} %bitcast.25, f32[]{:T(128)} %bitcast.24, f32[6]{0:T(128)S(1)} %multiply_reduce_fusion.1), kind=kLoop, calls=%fused_computation.63 | loop fusion | flops 18 | bytes 104 | tf_op jit(solution)/shard_map/jit(_where)/select_n | solution.py:342
  19.6 1.5 %fusion.1 = (bf16[4,4,72,512]{3,2,1,0:T(8,128)(2,1)S(1)}, bf16[4,4,72,512]{3,2,1,0:T(8,128)(2,1)S(1)}) fusion(s32[]{:T(128)S(6)} %select_n.151, bf16[2,4,4,72,256]{4,3,2,1,0:T(8,128)(2,1)S(1)} %bitcast.76, bf16[2,4,4,72,256]{4,3,2,1,0:T(8,128)(2,1)} %collective-permute-done, s32[]{:T(128)S(6)} %select_n.150), kind=kLoop, calls=%fused_computation.10 | loop fusion | flops 4718592 | bytes 4718600 | tf_op jit(solution)/shard_map/jit(dynamic_index_in_dim)/squeeze | solution.py:387
  21.1 39.0 %attend.1 = (bf16[4,4,72,512]{3,2,1,0:T(8,128)(2,1)S(1)}, bf16[2,4,72,512]{3,2,1,0:T(8,128)(2,1)S(1)}, f32[2,4,1,512]{3,2,1,0:T(1,128)S(1)}, f32[72,128]{1,0:T(8,128)S(1)}) custom-call(f32[1]{0:T(128)} %bitcast.5.far_ref, s32[3]{0:T(128)S(1)} %add_convert_fusion.flag_ref, bf16[4,4,72,512]{3,2,1,0:T(8,128)(2,1)S(1)} %get-tuple-element.35.a_ref, ...), custom_call_target="tpu_custom_call" | custom-call | tf_op jit(solution)/shard_map/attend/pallas_call | solution.py:282
  60.1 1.0 copy-done
  61.1 0.8 copy-done.2
  62.0 8.1 %gather.13 = f32[16,8,128]{2,1,0:T(8,128)S(1)} custom-call(f32[8,128]{1,0:T(8,128)S(1)} %pad.4.x_ref), custom_call_target="tpu_custom_call" | custom-call | tf_op jit(solution)/shard_map/gather/pallas_call | solution.py:322
  71.5 0.8 fusion.10
  73.3 1.2 %divide_reduce_fusion = f32[1152]{0:T(1024)S(1)} fusion(f32[6,1152]{1,0:T(8,128)S(1)} %get-tuple-element.49, s32[]{:T(128)S(6)} %select_n.159, f32[6,1152]{1,0:T(8,128)S(1)} %broadcast_divide_fusion.1, f32[1]{0:T(128)} %dynamic-slice.3, f32[1]{0:T(128)} %dynamic-slice.2), kind=kLoop, calls=%fused_computation.34 | loop fusion | flops 3456 | bytes 13836 | tf_op jit(solution)/shard_map/dynamic_slice | solution.py:402
  74.6 0.7 fusion.16
  75.5 1.3 %copy-done.1 = bf16[4,4,72,512]{3,2,1,0:T(8,128)(2,1)S(1)} copy-done((bf16[4,4,72,512]{3,2,1,0:T(8,128)(2,1)S(1)}, bf16[4,4,72,512]{3,2,1,0:T(8,128)(2,1)}, u32[]{:S(2)}) %copy-start.1) | copy-done | bytes 1179672
  76.8 1.1 copy-done.3
  77.8 29.9 %grads.1 = bf16[2,4,3,72,512]{4,3,2,1,0:T(8,128)(2,1)S(1)} custom-call(f32[1]{0:T(128)} %bitcast.5.far_ref, s32[3]{0:T(128)S(1)} %add_convert_fusion.flag_ref, bf16[4,4,72,512]{3,2,1,0:T(8,128)(2,1)S(1)} %get-tuple-element.35.a_ref, bf16[4,4,72,512]{3,2,1,0:T(8,128)(2,1)S(1)} %copy-done.1, bf16[2,4,72,512]{3,2,1,0:T(8,128)(2,1)S(1)} %copy-done.3, ...), custom_call_target="tpu_custom_call" | custom-call | tf_op jit(solution)/shard_map/grads/pallas_call | solution.py:303
  107.8 2.1 %collective-permute-start.1 = (bf16[2,4,3,72,256]{4,3,2,1,0:T(8,128)(2,1)S(1)}, bf16[2,4,3,72,256]{4,3,2,1,0:T(8,128)(2,1)}, u32[]{:S(2)}, u32[]{:S(2)}) collective-permute-start(bf16[2,4,3,72,256]{4,3,2,1,0:T(8,128)(2,1)S(1)} %slice.50), channel_id=1, source_target_pairs={{0,1},{1,0},{2,3},{3,2},{4,5},{5,4},{6,7},{7,6},{8,9},{9,8},{10,11... | collective-permute-start | bytes 2654216 | tf_op jit(solution)/shard_map/ppermute | solution.py:374
  109.9 2.2 %collective-permute-done.1 = bf16[2,4,3,72,256]{4,3,2,1,0:T(8,128)(2,1)} collective-permute-done((bf16[2,4,3,72,256]{4,3,2,1,0:T(8,128)(2,1)S(1)}, bf16[2,4,3,72,256]{4,3,2,1,0:T(8,128)(2,1)}, u32[]{:S(2)}, u32[]{:S(2)}) %collective-permute-start.1) | collective-permute-done | bytes 884768 | tf_op jit(solution)/shard_map/ppermute | solution.py:374
  112.1 1.3 %select_bitcast_fusion.1 = (bf16[2,1,4,3,72,256]{5,4,3,2,0,1:T(8,128)(2,1)S(1)}, bf16[2,1,4,3,72,256]{5,4,3,2,0,1:T(8,128)(2,1)S(1)}) fusion(bf16[2,4,3,72,256]{4,3,2,1,0:T(8,128)(2,1)} %collective-permute-done.1, pred[]{:T(512)S(6)} %eq.66, bf16[2,4,3,72,512]{4,3,2,1,0:T(8,128)(2,1)S(1)} %grads.1), kind=kLoop, calls=%fused_computation.19 | loop fusion | flops 884736 | bytes 3538945 | tf_op jit(solution)/shard_map/stack | solution.py:411
  113.8 1.1 copy.81
  114.9 1.1 copy.80
  116.0 1.1 copy.79
  (62 shorter events, 7.7 us)
Async XLA Ops:
  0.6 2.7 %copy-start.5 = (bf16[256,1152]{1,0:T(8,128)(2,1)S(1)}, bf16[256,1152]{1,0:T(8,128)(2,1)}, u32[]{:S(2)}) copy-start(bf16[256,1152]{1,0:T(8,128)(2,1)} %param.11) | copy-start | bytes 1769476
  0.7 3.0 %copy-start.6 = (bf16[256,1152]{1,0:T(8,128)(2,1)S(1)}, bf16[256,1152]{1,0:T(8,128)(2,1)}, u32[]{:S(2)}) copy-start(bf16[256,1152]{1,0:T(8,128)(2,1)} %param.12) | copy-start | bytes 1769476
  4.4 1.8 %copy-start.4 = (s32[6]{0:T(128)S(1)}, s32[6]{0:T(128)}, u32[]{:S(2)}) copy-start(s32[6]{0:T(128)} %param.13) | copy-start | bytes 76
  5.5 12.0 %copy-start.8 = (f32[2]{0:T(128)S(1)}, f32[2]{0:T(128)}, u32[]{:S(2)}) copy-start(f32[2]{0:T(128)} %param.17) | copy-start | bytes 28
  5.5 12.6 %copy-start.7 = (f32[6,1152]{1,0:T(8,128)S(1)}, f32[6,1152]{1,0:T(8,128)}, u32[]{:S(2)}) copy-start(f32[6,1152]{1,0:T(8,128)} %param.16) | copy-start | bytes 82948
  5.5 14.1 %collective-permute-start = (bf16[2,4,4,72,256]{4,3,2,1,0:T(8,128)(2,1)}, bf16[2,4,4,72,256]{4,3,2,1,0:T(8,128)(2,1)}, u32[]{:S(2)}, u32[]{:S(2)}) collective-permute-start(bf16[2,4,4,72,256]{4,3,2,1,0:T(8,128)(2,1)} %bitcast.69), channel_id=1, source_target_pairs={{0,1},{1,0},{2,3},{3,2},{4,5},{5,4},{6,7},{7,6},{8,9},{9,8},{10,11... | collective-permute-start | bytes 3538952 | tf_op jit(solution)/shard_map/ppermute | solution.py:374
  6.4 11.9 %copy-start.9 = (s32[6]{0:T(128)S(1)}, s32[6]{0:T(128)}, u32[]{:S(2)}) copy-start(s32[6]{0:T(128)} %param.14) | copy-start | bytes 76
  21.1 50.5 %copy-start.10 = (s32[6]{0:T(128)S(1)}, s32[6]{0:T(128)}, u32[]{:S(2)}) copy-start(s32[6]{0:T(128)} %param.15) | copy-start | bytes 76
  60.1 1.0 copy-start
  61.1 0.8 copy-start.2
  75.5 1.3 %copy-start.1 = (bf16[4,4,72,512]{3,2,1,0:T(8,128)(2,1)S(1)}, bf16[4,4,72,512]{3,2,1,0:T(8,128)(2,1)}, u32[]{:S(2)}) copy-start(bf16[4,4,72,512]{3,2,1,0:T(8,128)(2,1)} %copy-done) | copy-start | bytes 3538948
  76.8 1.1 copy-start.3
  107.8 4.3 %collective-permute-start.1 = (bf16[2,4,3,72,256]{4,3,2,1,0:T(8,128)(2,1)S(1)}, bf16[2,4,3,72,256]{4,3,2,1,0:T(8,128)(2,1)}, u32[]{:S(2)}, u32[]{:S(2)}) collective-permute-start(bf16[2,4,3,72,256]{4,3,2,1,0:T(8,128)(2,1)S(1)} %slice.50), channel_id=1, source_target_pairs={{0,1},{1,0},{2,3},{3,2},{4,5},{5,4},{6,7},{7,6},{8,9},{9,8},{10,11... | collective-permute-start | bytes 2654216 | tf_op jit(solution)/shard_map/ppermute | solution.py:374

commit v3 on v2

v3 whole, which is shorter than its diff:
```python
import jax
import jax.numpy as jnp
from jax import lax
from jax.experimental import pallas as pl
from jax.experimental.pallas import tpu as pltpu
from jax.sharding import PartitionSpec as P

HEADS = 16
HEAD_DIM = 72
BLOCK = 512
QUARTER = 4
CHUNK = 256
TEMPER = 10.0
LOSS_SCALE = 65536.0
EPSILON = 1e-06
SCALE = HEAD_DIM ** (-0.5)
LOG2E = 1.4426950408889634
FAR = -1e30


def dot_over(x, y, dim_x, dim_y):
    return lax.dot_general(
        x, y, (((dim_x,), (dim_y,)), ((), ())), preferred_element_type=jnp.float32
    )


def chosen(flag, x, y):
    return jnp.where(flag, x.astype(jnp.float32), y.astype(jnp.float32)).astype(jnp.bfloat16)


def step_kernel(
    lengths_ref, modality_ref, pairs_ref, bias_ref,
    q_ref, k_ref, v_ref, u_ref, texts_ref,
    gq_ref, gk_ref, gv_ref, loss_ref,
    send_ref, sendu_ref, near_ref, nearu_ref, relay_ref, relayu_ref, swap_ref,
    a_ref, b_ref, att_ref, lse_ref, note_ref, pools_ref, extra_ref,
    res_ref, back_ref, far_back_ref, swap_back_ref, acc_ref,
    swap_sems, near_sems, relay_sems, note_sems, back_sems, far_back_sems, swap_back_sems,
):
    devices = lax.axis_size("ctx")
    blocks = devices // 2
    count = texts_ref.shape[0]
    rows = BLOCK // 2
    me = lax.axis_index("ctx")
    core = me % 2
    block = me // 2
    odd = block % 2
    mate = me + 1 - 2 * core
    across = (block + 1 - 2 * odd) * 2
    target = me + 4 - 8 * odd
    source = me - 4 + 8 * odd
    has_target = (target >= 0) & (target < devices)
    has_source = (source >= 0) & (source < devices)

    barrier = pltpu.get_barrier_semaphore()

    def peer(step):
        return (me + step) % devices

    def greet_one(step, carry):
        pl.semaphore_signal(
            barrier, inc=1, device_id={"ctx": peer(step)}, device_id_type=pl.DeviceIdType.MESH
        )
        return carry

    lax.fori_loop(1, devices, greet_one, 0)

    def place_of(at):
        scene, start, length, end = 0, 0, 0, 0
        for s in range(count):
            begin = end
            end = end + lengths_ref[s]
            here = (at >= begin) & (at < end)
            scene = jnp.where(here, s, scene)
            start = jnp.where(here, begin, start)
            length = jnp.where(here, lengths_ref[s], length)
        return scene, at - start, length

    scene, second, length = place_of(block)
    paired = length == 2
    late = second == 1
    beside = (block + 1 - 2 * second) == (block + 1 - 2 * odd)
    far = jnp.where(paired, 0.0, FAR).astype(jnp.float32)
    inputs = (q_ref, k_ref, v_ref, u_ref)

    def remote(src, dst, send_sem, recv_sem, device):
        return pltpu.make_async_remote_copy(
            src_ref=src,
            dst_ref=dst,
            send_sem=send_sem,
            recv_sem=recv_sem,
            device_id={"ctx": device},
            device_id_type=pl.DeviceIdType.MESH,
        )

    def swap(kind):
        return remote(
            inputs[kind].at[:, 1 - core], swap_ref.at[kind],
            swap_sems.at[0, kind], swap_sems.at[1, kind], mate,
        )

    def near(h, to, slot):
        return remote(
            send_ref.at[to, h], near_ref.at[slot, h],
            near_sems.at[0, to, h], near_sems.at[1, slot, h], across + to,
        )

    def near_up(to, slot):
        return remote(
            sendu_ref.at[to], nearu_ref.at[slot],
            near_sems.at[0, to, QUARTER], near_sems.at[1, slot, QUARTER], across + to,
        )

    def relay(h, slot):
        return remote(
            near_ref.at[slot, h], relay_ref.at[slot, h],
            relay_sems.at[0, slot, h], relay_sems.at[1, slot, h], target,
        )

    def relay_up(slot):
        return remote(
            nearu_ref.at[slot], relayu_ref.at[slot],
            relay_sems.at[0, slot, QUARTER], relay_sems.at[1, slot, QUARTER], target,
        )

    def back(h, to, slot):
        return remote(
            res_ref.at[1, to, h], back_ref.at[slot, h],
            back_sems.at[0, to, h], back_sems.at[1, slot, h], across + to,
        )

    def far_back(h, slot):
        return remote(
            back_ref.at[slot, h], far_back_ref.at[slot, h],
            far_back_sems.at[0, slot, h], far_back_sems.at[1, slot, h], target,
        )

    def swap_back(h, side):
        return remote(
            res_ref.at[side, 1, h], swap_back_ref.at[side, h],
            swap_back_sems.at[0, side, h], swap_back_sems.at[1, side, h], mate,
        )

    @pl.when(jnp.logical_not(has_source))
    def _():
        relay_ref[...] = jnp.zeros_like(relay_ref)
        relayu_ref[...] = jnp.zeros_like(relayu_ref)
        far_back_ref[...] = jnp.zeros_like(far_back_ref)

    def fill(h, carry):
        for to in range(2):
            for kind in range(3):
                send_ref[to, h, kind] = chosen(
                    late, inputs[kind][0, to, h], inputs[kind][1, to, h]
                )
            sendu_ref[to, h] = chosen(late, u_ref[0, to, h], u_ref[1, to, h])
        return carry

    lax.fori_loop(0, QUARTER, fill, 0)
    pl.semaphore_wait(barrier, devices - 1)
    for h in range(QUARTER):
        for to in range(2):
            near(h, to, core).start()
        swap(h).start()
    for to in range(2):
        near_up(to, core).start()

    def pass_on(h):
        for slot in range(2):
            near(h, slot, slot).wait_recv()
        for slot in range(2):
            pl.when(has_target)(lambda slot=slot: relay(h, slot).start())

    for kind in range(4):
        swap(kind).wait_recv()
    pass_on(0)
    lane = lax.broadcasted_iota(jnp.int32, (HEAD_DIM, 128), 1)
    sides = (a_ref, b_ref)

    def own_tiles(h, kind, near_pair, relay_pair):
        x = inputs[kind]
        low, high = x[0, core, h], x[1, core, h]
        low_far, high_far = swap_ref[kind, 0, h], swap_ref[kind, 1, h]
        a_ref[h, kind, :, :rows] = chosen(late, high, low)
        a_ref[h, kind, :, rows:] = chosen(late, high_far, low_far)
        for slot, alone in ((0, high), (1, high_far)):
            b_ref[h, kind, :, slot * rows : (slot + 1) * rows] = chosen(
                paired, chosen(beside, near_pair[slot], relay_pair[slot]), alone
            )

    def one_head(h, gathered):
        pl.when(h < QUARTER - 1)(lambda: pass_on(h + 1))

        @pl.when(has_source)
        def _():
            for slot in range(2):
                relay(h, slot).wait_recv()

        for kind in range(3):
            own_tiles(
                h, kind,
                [near_ref[slot, h, kind] for slot in range(2)],
                [relay_ref[slot, h, kind] for slot in range(2)],
            )
        for own in range(2):
            pool = jnp.zeros((HEAD_DIM, 1), jnp.float32)
            for start in range(0, BLOCK, CHUNK):
                q = sides[own][h, 0, :, start : start + CHUNK]
                scores = []
                for side in range(2):
                    s = dot_over(sides[side][h, 1], q, 0, 0) * (SCALE * LOG2E)
                    scores.append(s if side == own else s + far)
                top = jnp.maximum(
                    jnp.max(scores[0], axis=0, keepdims=True),
                    jnp.max(scores[1], axis=0, keepdims=True),
                )
                parts = [jnp.exp2(s - top) for s in scores]
                total = jnp.sum(parts[0], axis=0, keepdims=True) + jnp.sum(
                    parts[1], axis=0, keepdims=True
                )
                scale = 1.0 / total
                att = jnp.zeros((HEAD_DIM, CHUNK), jnp.float32)
                for side in range(2):
                    probs = (parts[side] * scale).astype(jnp.bfloat16)
                    att = att + dot_over(sides[side][h, 2], probs, 1, 0)
                att = att.astype(jnp.bfloat16)
                att_ref[own, h, :, start : start + CHUNK] = att
                lse_ref[own, h, :, start : start + CHUNK] = top + jnp.log2(total)
                pool = pool + jnp.sum(att.astype(jnp.float32), axis=1, keepdims=True)
            gathered = jnp.where(lane == own * QUARTER + h, pool, gathered)
        return gathered

    pool = lax.fori_loop(0, QUARTER, one_head, jnp.zeros((HEAD_DIM, 128), jnp.float32))
    pool = jnp.concatenate([pool, jnp.zeros((128 - HEAD_DIM, 128), jnp.float32)], axis=0)
    note_ref[...] = pool.T[: 2 * QUARTER]

    def note(step, slot):
        return remote(
            note_ref, pools_ref.at[slot], note_sems.at[0, step], note_sems.at[1, step], peer(step)
        )

    def send_note(step, carry):
        note(step, me).start()
        return carry

    lax.fori_loop(1, devices, send_note, 0)
    pools_ref[me] = note_ref[...]
    for slot in range(2):
        near_up(slot, slot).wait_recv()
    for slot in range(2):
        pl.when(has_target)(lambda slot=slot: relay_up(slot).start())

    text = texts_ref[...]

    def total_of(x):
        return jnp.sum(jnp.sum(x, axis=2, keepdims=True), axis=1, keepdims=True)

    text_unit = text / jnp.sqrt(total_of(text * text) + EPSILON)
    which = lax.broadcasted_iota(jnp.int32, (count, 1, 1), 0)
    which_full = lax.broadcasted_iota(jnp.int32, (count, 16, 128), 0)
    row_half = lax.broadcasted_iota(jnp.int32, (8, 128), 0) // QUARTER

    def wait_note(step, carry):
        done = note(step, (me + devices - step) % devices)
        done.wait_recv()
        done.wait_send()
        return carry

    lax.fori_loop(1, devices, wait_note, 0)

    def add_block(at, sums):
        its_scene, its_second, its_length = place_of(at)
        pieces = []
        for its_core in range(2):
            x = pools_ref[2 * at + its_core]
            both = x + jnp.concatenate([x[QUARTER:], x[:QUARTER]], axis=0)
            both = jnp.where(row_half == its_second, both, 0.0)
            pieces.append(jnp.where(its_length == 2, both, x))
        piece = jnp.concatenate(pieces, axis=0)
        return sums + jnp.where(which_full == its_scene, piece[None], 0.0)

    sums = lax.fori_loop(0, blocks, add_block, jnp.zeros((count, 16, 128), jnp.float32))
    sizes = jnp.zeros((count, 1, 1), jnp.float32)
    for s in range(count):
        sizes = jnp.where(which == s, (lengths_ref[s] * BLOCK).astype(jnp.float32), sizes)
    pooled = sums / sizes
    norm = jnp.sqrt(total_of(pooled * pooled) + EPSILON)
    unit = pooled / norm
    loss = jnp.zeros((8, 128), jnp.float32)
    loss_lane = lax.broadcasted_iota(jnp.int32, (8, 128), 1)
    grad_logits = jnp.zeros((count, 1, 1), jnp.float32)
    for i in range(count):
        bias = jnp.where(modality_ref[i] == 0, bias_ref[0], bias_ref[1])
        logits = TEMPER * total_of(text_unit * unit[i : i + 1]) + bias
        label = jnp.where(which == pairs_ref[i], 1.0, -1.0)
        margin = label * logits
        plus = jnp.maximum(-margin, 0.0) + jnp.log1p(jnp.exp(-jnp.abs(margin)))
        loss = jnp.where(loss_lane == i, jnp.sum(plus, axis=0), loss)
        slope = -label / (1.0 + jnp.exp(margin)) * (LOSS_SCALE / count)
        grad_logits = jnp.where(scene == i, slope, grad_logits)
    loss_ref[...] = loss
    grad_unit = TEMPER * jnp.sum(grad_logits * text_unit, axis=0, keepdims=True)
    mine = which == scene
    my_unit = jnp.sum(jnp.where(which_full == scene, unit, 0.0), axis=0, keepdims=True)
    my_norm = jnp.sum(jnp.where(mine, norm, 0.0), axis=0, keepdims=True)
    my_size = (length * BLOCK).astype(jnp.float32)
    grad_pooled = (grad_unit - my_unit * total_of(my_unit * grad_unit)) / my_norm
    per_token = (grad_pooled / my_size)[0]
    per_core = jnp.where(core == 0, per_token[:8], per_token[8:])
    columns = jnp.concatenate([per_core, jnp.zeros((120, 128), jnp.float32)], axis=0).T
    for h in range(QUARTER):
        low = columns[:HEAD_DIM, h : h + 1]
        high = columns[:HEAD_DIM, QUARTER + h : QUARTER + h + 1]
        own = jnp.where(late, high, low)
        extra_ref[0, h] = own
        extra_ref[1, h] = jnp.where(paired, own, high)

    @pl.when(has_source)
    def _():
        for slot in range(2):
            relay_up(slot).wait_recv()

    def pass_back(h):
        for slot in range(2):
            back(h, slot, slot).wait_recv()
        for slot in range(2):
            pl.when(has_target)(lambda slot=slot: far_back(h, slot).start())

    def one_grad(h, carry):
        own_tiles(
            h, 3,
            [nearu_ref[slot, h] for slot in range(2)],
            [relayu_ref[slot, h] for slot in range(2)],
        )
        first = True
        for own in range(2):
            for start in range(0, BLOCK, CHUNK):
                span = slice(start, start + CHUNK)
                q = sides[own][h, 0, :, span]
                up = sides[own][h, 3, :, span].astype(jnp.float32)
                grad = (up + extra_ref[own, h]).astype(jnp.bfloat16)
                att = att_ref[own, h, :, span].astype(jnp.float32)
                lse = lse_ref[own, h, :, span]
                delta = jnp.sum(grad.astype(jnp.float32) * att, axis=0, keepdims=True)
                grad_q = jnp.zeros((HEAD_DIM, CHUNK), jnp.float32)
                for side in range(2):
                    k = sides[side][h, 1]
                    s = dot_over(k, q, 0, 0) * (SCALE * LOG2E)
                    if side != own:
                        s = s + far
                    probs = jnp.exp2(s - lse)
                    grad_probs = dot_over(sides[side][h, 2], grad, 0, 0)
                    grad_scores = (probs * (grad_probs - delta)).astype(jnp.bfloat16)
                    grad_q = grad_q + dot_over(k, grad_scores, 1, 0)
                    grad_k = dot_over(q, grad_scores, 1, 1)
                    grad_v = dot_over(grad, probs.astype(jnp.bfloat16), 1, 1)
                    if first:
                        acc_ref[side, 0] = grad_k
                        acc_ref[side, 1] = grad_v
                    else:
                        acc_ref[side, 0] += grad_k
                        acc_ref[side, 1] += grad_v
                first = False
                res_ref[own, start // CHUNK, h, 0] = (grad_q * SCALE).astype(jnp.bfloat16)
        for side in range(2):
            for part in range(2):
                span = slice(part * rows, (part + 1) * rows)
                res_ref[side, part, h, 1] = (acc_ref[side, 0, :, span] * SCALE).astype(
                    jnp.bfloat16
                )
                res_ref[side, part, h, 2] = acc_ref[side, 1, :, span].astype(jnp.bfloat16)
        for to in range(2):
            back(h, to, core).start()
        for side in range(2):
            swap_back(h, side).start()
        pl.when(h > 0)(lambda: pass_back(h - 1))
        return carry

    lax.fori_loop(0, QUARTER, one_grad, 0)
    pass_back(QUARTER - 1)
    outs = (gq_ref, gk_ref, gv_ref)

    def settle(h, carry):
        for side in range(2):
            swap_back(h, side).wait_recv()

        @pl.when(has_source)
        def _():
            for slot in range(2):
                far_back(h, slot).wait_recv()

        for kind in range(3):
            for its_core, own, alone in (
                (core, res_ref[0, 0, h, kind], res_ref[1, 0, h, kind]),
                (1 - core, swap_back_ref[0, h, kind], swap_back_ref[1, h, kind]),
            ):
                came = chosen(
                    beside, back_ref[its_core, h, kind], far_back_ref[its_core, h, kind]
                )
                other = chosen(paired, came, alone)
                outs[kind][0, its_core, h] = chosen(late, other, own)
                outs[kind][1, its_core, h] = chosen(late, own, other)
        return carry

    lax.fori_loop(0, QUARTER, settle, 0)
    for kind in range(4):
        swap(kind).wait_send()
    for to in range(2):
        near_up(to, core).wait_send()
        pl.when(has_target)(lambda to=to: relay_up(to).wait_send())

    def drain(h, carry):
        for to in range(2):
            near(h, to, core).wait_send()
            back(h, to, core).wait_send()
            swap_back(h, to).wait_send()

        @pl.when(has_target)
        def _():
            for slot in range(2):
                relay(h, slot).wait_send()
                far_back(h, slot).wait_send()

        return carry

    lax.fori_loop(0, QUARTER, drain, 0)


SMEM = pl.BlockSpec(memory_space=pltpu.SMEM)
VMEM = pl.BlockSpec(memory_space=pltpu.VMEM)


def on_device(queries, keys, values, upstream, lengths, modality, pairs, texts, modality_bias):
    rows = queries.shape[0]
    devices = lax.axis_size("ctx")
    count = lengths.shape[0]
    assert rows * 2 == BLOCK
    xs = [x.T.reshape(2, 2, QUARTER, HEAD_DIM, rows) for x in (queries, keys, values, upstream)]
    text = texts.reshape(count, 2, 2, QUARTER, HEAD_DIM).transpose(0, 2, 1, 3, 4)
    text = jnp.pad(text.reshape(count, HEADS, HEAD_DIM), ((0, 0), (0, 0), (0, 128 - HEAD_DIM)))
    bf16, f32 = jnp.bfloat16, jnp.float32
    tile = (HEAD_DIM, rows)
    wide = (HEAD_DIM, BLOCK)
    dma = pltpu.SemaphoreType.DMA
    shaped = jax.ShapeDtypeStruct((2, 2, QUARTER) + tile, bf16)
    gq, gk, gv, loss = pl.pallas_call(
        step_kernel,
        in_specs=[SMEM] * 4 + [VMEM] * 5,
        out_specs=[VMEM] * 4,
        out_shape=[shaped, shaped, shaped, jax.ShapeDtypeStruct((8, 128), f32)],
        scratch_shapes=[
            pltpu.VMEM((2, QUARTER, 3) + tile, bf16),
            pltpu.VMEM((2, QUARTER) + tile, bf16),
            pltpu.VMEM((2, QUARTER, 3) + tile, bf16),
            pltpu.VMEM((2, QUARTER) + tile, bf16),
            pltpu.VMEM((2, QUARTER, 3) + tile, bf16),
            pltpu.VMEM((2, QUARTER) + tile, bf16),
            pltpu.VMEM((4, 2, QUARTER) + tile, bf16),
            pltpu.VMEM((QUARTER, 4) + wide, bf16),
            pltpu.VMEM((QUARTER, 4) + wide, bf16),
            pltpu.VMEM((2, QUARTER) + wide, bf16),
            pltpu.VMEM((2, QUARTER, 1, BLOCK), f32),
            pltpu.VMEM((8, 128), f32),
            pltpu.VMEM((devices, 8, 128), f32),
            pltpu.VMEM((2, QUARTER, HEAD_DIM, 1), f32),
            pltpu.VMEM((2, 2, QUARTER, 3) + tile, bf16),
            pltpu.VMEM((2, QUARTER, 3) + tile, bf16),
            pltpu.VMEM((2, QUARTER, 3) + tile, bf16),
            pltpu.VMEM((2, QUARTER, 3) + tile, bf16),
            pltpu.VMEM((2, 2) + wide, f32),
            dma((2, 4)),
            dma((2, 2, QUARTER + 1)),
            dma((2, 2, QUARTER + 1)),
            dma((2, devices)),
            dma((2, 2, QUARTER)),
            dma((2, 2, QUARTER)),
            dma((2, 2, QUARTER)),
        ],
        compiler_params=pltpu.CompilerParams(
            vmem_limit_bytes=48 * 2**20, collective_id=0, has_side_effects=True
        ),
        name="scene_step",
    )(lengths, modality, pairs, modality_bias, *xs, text)
    back = [g.reshape(HEADS * HEAD_DIM, rows).T for g in (gq, gk, gv)]
    return back[0], back[1], back[2], loss[0, :count]


def solution(mesh):
    tokens = P(("groups", "ctx"), None)
    in_specs = (
        tokens, tokens, tokens, tokens,
        P("groups"), P("groups"), P("groups"), P("groups", None), P(),
    )
    out_specs = (tokens, tokens, tokens, P("groups"))
    return jax.shard_map(
        on_device, mesh=mesh, in_specs=in_specs, out_specs=out_specs, check_vma=False
    )
```

time: 118 us -> 84.9 us (0.72)
  other arithmetic: 8.12 us -> 0 us
  between operations: 8.13 us -> 0.73 us
  Pallas kernels: 77 us -> 71 us
  local copies, waits for them, and re-layouts: 17.6 us -> 12.3 us
  starting transfers between devices: 2.79 us -> 0 us
  waiting for transfers between devices: 2.19 us -> 0 us
  matrix products: 1.19 us -> 0 us
    unnamed x29 -> x18, local copies, waits for them, and re-layouts: 10.5 us -> 3.9 us
    pallas_call x3 -> x1, Pallas kernels: 77 us -> 71 us  [on_device(): pl.pallas_call(step_kernel, in_specs=[SMEM] * 4 + [VMEM] * 5, out_specs=[...]
    reshape x1 -> x5, local copies, waits for them, and re-layouts: 0.12 us -> 5.12 us  [the longest x3 4.23 us: on_device(): back = [g.reshape(HEADS * HEAD_DIM, rows).T for g in (gq, gk, gv)]]
    dynamic_slice x8 -> x0, local copies, waits for them, and re-layouts: 4.32 us -> none  [the longest x3 1.76 us: on_device(): scene, second, paired = (scenes[block], seconds[block], paired_at[block])]
    ppermute x2 -> x0, starting transfers between devices: 2.79 us -> none  [swap_core(): return lax.ppermute(x, 'ctx', [(i, i ^ 1) for i in range(devices)])]
    ppermute x2 -> x0, waiting for transfers between devices: 2.19 us -> none  [swap_core(): return lax.ppermute(x, 'ctx', [(i, i ^ 1) for i in range(devices)])]
    transpose x1 -> x4, local copies, waits for them, and re-layouts: 0.01 us -> 2.1 us  [on_device(): x.T.reshape(2, 2, QUARTER, HEAD_DIM, rows)]
    select_n x4 -> x0, other arithmetic: 2.07 us -> none  [the longest x1 1.3 us: contrast(): bias = jnp.where(modality == 0, modality_bias[0], modality_bias[1])]
  transfers between devices with their start and end apart: 2 -> 0, of which waited for: 1 -> 0; matrix products, arithmetic and copies ran while one was open for 5% -> 0% of each run, Pallas kernels for 0% -> 0%
where the time goes in v3:
time: 84.9 us; the launch traced here: 83.9 us
  Pallas kernels  71 us (84%)
  local copies, waits for them, and re-layouts  12.3 us (14%)
    pallas_call x1, Pallas kernels, on_device(): pl.pallas_call(step_kernel, in_specs=[SMEM] * 4 + [VMEM] * 5, out_specs=[...  71 us
    reshape x3, local copies, waits for them, and re-layouts, on_device(): back = [g.reshape(HEADS * HEAD_DIM, rows).T for g in (gq, gk, gv)]  4.23 us
    unnamed x18, local copies, waits for them, and re-layouts  3.9 us
    transpose x4, local copies, waits for them, and re-layouts, on_device(): x.T.reshape(2, 2, QUARTER, HEAD_DIM, rows)  2.1 us

profile of v3, /device:TPU:25, one launch (start us, length us, event | category | flops | bytes accessed | tf_op | source)
XLA Modules:
  0.0 83.9 jit_solution(14840020883592727910)
XLA Ops:
  0.6 0.9 %reshape.39 = f32[6,2,2,4,72]{4,3,2,1,0:T(4,128)S(1)} reshape(f32[6,1152]{1,0:T(8,128)} %param.16) | data formatting | bytes 55296 | tf_op jit(solution)/shard_map/reshape | solution.py:439
  1.5 0.6 pad.4.texts_ref
  2.2 1.4 %copy.13 = bf16[1152,256]{1,0:T(8,128)(2,1)S(1)} copy(bf16[1152,256]{0,1:T(8,128)(2,1)} %bitcast.26) | data formatting | bytes 1179648 | tf_op jit(solution)/shard_map/transpose | solution.py:438
  3.5 0.0 copy-start.7
  3.6 0.2 copy.14
  3.8 0.8 copy-done.7
  4.6 0.2 copy.15
  4.9 0.8 copy-done.8
  5.7 0.2 copy.16
  5.9 0.0 copy-start.2
  5.9 0.0 copy-start.3
  6.0 0.0 copy-start.4
  6.0 0.4 copy-done.5
  6.3 0.3 copy-done.2
  6.6 0.0 copy-done.3
  6.6 0.0 copy-done.4
  6.6 0.8 copy-done.1
  7.4 71.0 %scene_step.1 = (bf16[2,2,4,72,256]{4,3,2,1,0:T(8,128)(2,1)S(1)}, bf16[2,2,4,72,256]{4,3,2,1,0:T(8,128)(2,1)S(1)}, bf16[2,2,4,72,256]{4,3,2,1,0:T(8,128)(2,1)S(1)}, f32[8,128]{1,0:T(8,128)S(1)}) custom-call(s32[6]{0:T(128)S(1)} %copy-done.2, s32[6]{0:T(128)S(1)} %copy-done.3, s32[6]{0:T(128)S(1)} %copy-done.4, f32[2]{0:T(128)S(1)} %copy-done.5, ...), custom_call_target="tpu_custom_call" | custom-call | tf_op jit(solution)/shard_map/scene_step/pallas_call | solution.py:446
  78.4 0.0 copy-start
  78.4 0.8 copy-done
  79.2 2.1 %copy.18 = bf16[1152,256]{0,1:T(8,128)(2,1)} copy(bf16[1152,256]{1,0:T(8,128)(2,1)} %bitcast.25) | data formatting | bytes 1179648 | tf_op jit(solution)/shard_map/reshape | solution.py:484
  81.3 1.1 %copy.19 = bf16[1152,256]{0,1:T(8,128)(2,1)} copy(bf16[1152,256]{1,0:T(8,128)(2,1)S(1)} %bitcast.24) | data formatting | bytes 1179648 | tf_op jit(solution)/shard_map/reshape | solution.py:484
  82.4 0.5 slice_bitcast_fusion
  82.9 1.1 %copy.20 = bf16[1152,256]{0,1:T(8,128)(2,1)} copy(bf16[1152,256]{1,0:T(8,128)(2,1)S(1)} %bitcast.23) | data formatting | bytes 1179648 | tf_op jit(solution)/shard_map/reshape | solution.py:484
  (6 shorter events, 0.0 us)
Async XLA Ops:
  2.2 1.4 %copy-start.6 = (bf16[256,1152]{1,0:T(8,128)(2,1)S(1)}, bf16[256,1152]{1,0:T(8,128)(2,1)}, u32[]{:S(2)}) copy-start(bf16[256,1152]{1,0:T(8,128)(2,1)} %param.10) | copy-start | bytes 1769476
  3.5 1.1 %copy-start.7 = (bf16[256,1152]{1,0:T(8,128)(2,1)S(1)}, bf16[256,1152]{1,0:T(8,128)(2,1)}, u32[]{:S(2)}) copy-start(bf16[256,1152]{1,0:T(8,128)(2,1)} %param.11) | copy-start | bytes 1769476
  4.6 1.1 %copy-start.8 = (bf16[256,1152]{1,0:T(8,128)(2,1)S(1)}, bf16[256,1152]{1,0:T(8,128)(2,1)}, u32[]{:S(2)}) copy-start(bf16[256,1152]{1,0:T(8,128)(2,1)} %param.12) | copy-start | bytes 1769476
  5.7 0.7 copy-start.5
  5.9 0.7 copy-start.2
  5.9 0.7 copy-start.3
  6.0 0.7 copy-start.4
  6.6 0.8 copy-start.1
  78.4 0.8 copy-start

commit v4 on v3

--- a/solution.py
+++ b/solution.py
@@ -32,7 +32,7 @@
     lengths_ref, modality_ref, pairs_ref, bias_ref,
     q_ref, k_ref, v_ref, u_ref, texts_ref,
     gq_ref, gk_ref, gv_ref, loss_ref,
-    send_ref, sendu_ref, near_ref, nearu_ref, relay_ref, relayu_ref, swap_ref,
+    place_ref, send_ref, sendu_ref, near_ref, nearu_ref, relay_ref, relayu_ref, swap_ref,
     a_ref, b_ref, att_ref, lse_ref, note_ref, pools_ref, extra_ref,
     res_ref, back_ref, far_back_ref, swap_back_ref, acc_ref,
     swap_sems, near_sems, relay_sems, note_sems, back_sems, far_back_sems, swap_back_sems,
@@ -158,22 +158,37 @@
 
     lax.fori_loop(0, QUARTER, fill, 0)
     pl.semaphore_wait(barrier, devices - 1)
-    for h in range(QUARTER):
+    for h in range(2):
         for to in range(2):
             near(h, to, core).start()
-        swap(h).start()
-    for to in range(2):
-        near_up(to, core).start()
+    for kind in range(4):
+        swap(kind).start()
 
     def pass_on(h):
         for slot in range(2):
             near(h, slot, slot).wait_recv()
+
+        @pl.when(h < QUARTER - 2)
+        def _():
+            for to in range(2):
+                near(h + 2, to, core).start()
+
+        @pl.when(h == QUARTER - 2)
+        def _():
+            for to in range(2):
+                near_up(to, core).start()
+
         for slot in range(2):
             pl.when(has_target)(lambda slot=slot: relay(h, slot).start())
 
+    place_ref[...] = jnp.zeros_like(place_ref)
+    for row in range(HEADS):
+        half, its_core, h = row // 8, (row // 4) % 2, row % 4
+        piece = texts_ref[:, row * HEAD_DIM : (row + 1) * HEAD_DIM]
+        place_ref[:, its_core * 8 + half * 4 + h, :HEAD_DIM] = piece
     for kind in range(4):
         swap(kind).wait_recv()
-    pass_on(0)
+    lax.fori_loop(0, 1, lambda h, carry: (pass_on(h), carry)[1], 0)
     lane = lax.broadcasted_iota(jnp.int32, (HEAD_DIM, 128), 1)
     sides = (a_ref, b_ref)
 
@@ -250,7 +265,7 @@
     for slot in range(2):
         pl.when(has_target)(lambda slot=slot: relay_up(slot).start())
 
-    text = texts_ref[...]
+    text = place_ref[...]
 
     def total_of(x):
         return jnp.sum(jnp.sum(x, axis=2, keepdims=True), axis=1, keepdims=True)
@@ -436,8 +451,6 @@
     count = lengths.shape[0]
     assert rows * 2 == BLOCK
     xs = [x.T.reshape(2, 2, QUARTER, HEAD_DIM, rows) for x in (queries, keys, values, upstream)]
-    text = texts.reshape(count, 2, 2, QUARTER, HEAD_DIM).transpose(0, 2, 1, 3, 4)
-    text = jnp.pad(text.reshape(count, HEADS, HEAD_DIM), ((0, 0), (0, 0), (0, 128 - HEAD_DIM)))
     bf16, f32 = jnp.bfloat16, jnp.float32
     tile = (HEAD_DIM, rows)
     wide = (HEAD_DIM, BLOCK)
@@ -449,6 +462,7 @@
         out_specs=[VMEM] * 4,
         out_shape=[shaped, shaped, shaped, jax.ShapeDtypeStruct((8, 128), f32)],
         scratch_shapes=[
+            pltpu.VMEM((count, HEADS, 128), f32),
             pltpu.VMEM((2, QUARTER, 3) + tile, bf16),
             pltpu.VMEM((2, QUARTER) + tile, bf16),
             pltpu.VMEM((2, QUARTER, 3) + tile, bf16),
@@ -480,7 +494,7 @@
             vmem_limit_bytes=48 * 2**20, collective_id=0, has_side_effects=True
         ),
         name="scene_step",
-    )(lengths, modality, pairs, modality_bias, *xs, text)
+    )(lengths, modality, pairs, modality_bias, *xs, texts)
     back = [g.reshape(HEADS * HEAD_DIM, rows).T for g in (gq, gk, gv)]
     return back[0], back[1], back[2], loss[0, :count]
 

time: 84.9 us -> 83.3 us (0.981)
  local copies, waits for them, and re-layouts: 12.3 us -> 10.7 us
    reshape x2 -> x0, local copies, waits for them, and re-layouts: 0.9 us -> none  [on_device(): texts.reshape(count, 2, 2, QUARTER, HEAD_DIM).transpose(0, 2, 1, 3, 4)]
where the time goes in v4:
time: 83.3 us; the launch traced here: 82.4 us
  Pallas kernels  71 us (85%)
  local copies, waits for them, and re-layouts  10.7 us (13%)
    pallas_call x1, Pallas kernels, on_device(): pl.pallas_call(step_kernel, in_specs=[SMEM] * 4 + [VMEM] * 5, out_specs=[...  71 us
    reshape x3, local copies, waits for them, and re-layouts, on_device(): back = [g.reshape(HEADS * HEAD_DIM, rows).T for g in (gq, gk, gv)]  4.23 us
    unnamed x18, local copies, waits for them, and re-layouts  3.87 us
    transpose x4, local copies, waits for them, and re-layouts, on_device(): x.T.reshape(2, 2, QUARTER, HEAD_DIM, rows)  2.1 us

profile of v4, /device:TPU:25, one launch (start us, length us, event | category | flops | bytes accessed | tf_op | source)
XLA Modules:
  0.0 82.4 jit_solution(4877868112526820131)
XLA Ops:
  0.6 0.0 copy-start.6
  0.6 1.4 %copy.13 = bf16[1152,256]{1,0:T(8,128)(2,1)S(1)} copy(bf16[1152,256]{0,1:T(8,128)(2,1)} %bitcast.23) | data formatting | bytes 1179648 | tf_op jit(solution)/shard_map/transpose | solution.py:453
  2.0 0.0 copy-done.6
  2.0 0.0 copy-start.7
  2.0 0.2 copy.14
  2.3 0.8 copy-done.7
  3.1 0.2 copy.15
  3.3 0.8 copy-done.8
  4.2 0.2 copy.16
  4.4 0.0 copy-start.2
  4.4 0.0 copy-start.3
  4.4 0.0 copy-start.4
  4.4 0.4 copy-done.5
  4.8 0.3 copy-done.2
  5.1 0.0 copy-done.3
  5.1 0.0 copy-done.4
  5.1 0.8 copy-done.1
  5.9 71.0 %scene_step.1 = (bf16[2,2,4,72,256]{4,3,2,1,0:T(8,128)(2,1)S(1)}, bf16[2,2,4,72,256]{4,3,2,1,0:T(8,128)(2,1)S(1)}, bf16[2,2,4,72,256]{4,3,2,1,0:T(8,128)(2,1)S(1)}, f32[8,128]{1,0:T(8,128)S(1)}) custom-call(s32[6]{0:T(128)S(1)} %copy-done.2, s32[6]{0:T(128)S(1)} %copy-done.3, s32[6]{0:T(128)S(1)} %copy-done.4, f32[2]{0:T(128)S(1)} %copy-done.5, ...), custom_call_target="tpu_custom_call" | custom-call | tf_op jit(solution)/shard_map/scene_step/pallas_call | solution.py:459
  76.8 0.0 copy-start
  76.8 0.8 copy-done
  77.6 2.1 %copy.17 = bf16[1152,256]{0,1:T(8,128)(2,1)} copy(bf16[1152,256]{1,0:T(8,128)(2,1)} %bitcast.22) | data formatting | bytes 1179648 | tf_op jit(solution)/shard_map/reshape | solution.py:498
  79.8 1.1 %copy.18 = bf16[1152,256]{0,1:T(8,128)(2,1)} copy(bf16[1152,256]{1,0:T(8,128)(2,1)S(1)} %bitcast.21) | data formatting | bytes 1179648 | tf_op jit(solution)/shard_map/reshape | solution.py:498
  80.8 0.5 slice_bitcast_fusion
  81.3 1.1 %copy.19 = bf16[1152,256]{0,1:T(8,128)(2,1)} copy(bf16[1152,256]{1,0:T(8,128)(2,1)S(1)} %bitcast.20) | data formatting | bytes 1179648 | tf_op jit(solution)/shard_map/reshape | solution.py:498
  (3 shorter events, 0.0 us)
Async XLA Ops:
  0.6 1.4 %copy-start.6 = (bf16[256,1152]{1,0:T(8,128)(2,1)S(1)}, bf16[256,1152]{1,0:T(8,128)(2,1)}, u32[]{:S(2)}) copy-start(bf16[256,1152]{1,0:T(8,128)(2,1)} %param.10) | copy-start | bytes 1769476
  2.0 1.1 %copy-start.7 = (bf16[256,1152]{1,0:T(8,128)(2,1)S(1)}, bf16[256,1152]{1,0:T(8,128)(2,1)}, u32[]{:S(2)}) copy-start(bf16[256,1152]{1,0:T(8,128)(2,1)} %param.11) | copy-start | bytes 1769476
  3.1 1.1 %copy-start.8 = (bf16[256,1152]{1,0:T(8,128)(2,1)S(1)}, bf16[256,1152]{1,0:T(8,128)(2,1)}, u32[]{:S(2)}) copy-start(bf16[256,1152]{1,0:T(8,128)(2,1)} %param.12) | copy-start | bytes 1769476
  4.1 0.7 copy-start.5
  4.4 0.7 copy-start.2
  4.4 0.7 copy-start.3
  4.4 0.7 copy-start.4
  5.1 0.8 copy-start.1
  76.8 0.8 copy-start
